TPU v7x, 128 devices: a whole 4x4x4 slice. The times are simulated.
128 devices in a mesh: cp: 32 (over z, y_hi, x), tp: 4 (over y_lo, core).
Axes of the slice: x: 4, y: 4 (y_hi: 2, y_lo: 2; y = y_hi * 2 + y_lo), z: 4, core: 2. Of those that a mesh axis runs over, the one named last changes fastest.
Arguments:
- queries: bfloat16 [256, 128, 128], P('cp', 'tp'), may hold values from -32 to 32
- keys: bfloat16 [65536, 8, 128], P('cp', 'tp'), may hold values from -24 to 24
- values: bfloat16 [65536, 8, 128], P('cp', 'tp'), may hold values from -12 to 12
- lengths: int32 [32], P('cp'), may hold values from 1024 to 2048
- start: int32 [1], replicated, may hold values from 32512 to 65280
- out_weight: bfloat16 [16384, 16384], P('tp', 'cp'), may hold values from -0.046875 to 0.046875
Outputs:
- projected: bfloat16 [256, 16384], P('tp', 'cp')
All inputs are finite; a program needn't handle non-finite values.
Results may differ from a plain program's by a relative error of at most 0.0065.
Values may be sent and summed in bfloat16 or wider, within the bound.
No kernel may reach another device: no remote copies, remote signals or barrier semaphores. Data moves between devices by JAX's collectives and lax.ppermute only.
A program may use at most 64 MiB of HBM per device.

v0:
```python
import functools
import itertools
import math

import jax
import jax.numpy as jnp
from jax import lax
from jax.experimental import pallas as pl
from jax.experimental.pallas import tpu as pltpu
from jax.sharding import PartitionSpec as P

NEG = -1e30
BIG = 2.0**100
RING = 4
MIB = 2**20


def coords(cp, tp):
    z, yh, x = cp // 8, (cp // 4) % 2, cp % 4
    yl, core = tp // 2, tp % 2
    return z, yh, x, yl, core


def moved(x, a=0, b=0, yh=0, yl=0, core=0):
    pairs = []
    for cp, tp in itertools.product(range(32), range(4)):
        zi, yhi, xi, yli, ci = coords(cp, tp)
        dz, dx = (a, b) if ci == 0 else (b, a)
        zo, xo = (zi + dz) % RING, (xi + dx) % RING
        yho, ylo, co = yhi ^ yh, yli ^ yl, ci ^ core
        pairs.append((cp * 4 + tp, ((zo * 2 + yho) * 4 + xo) * 4 + ylo * 2 + co))
    return lax.ppermute(x, ("cp", "tp"), pairs)


def together(*arrays):
    return lax.optimization_barrier(arrays)


def source(me, da, db, dy):
    z, yh, x, _, core = me
    dz = jnp.where(core == 0, da, db)
    dx = jnp.where(core == 0, db, da)
    return (z - dz) & (RING - 1), yh ^ dy, (x - dx) & (RING - 1)


def spread(row, eye):
    return jnp.sum(jnp.where(eye, row, 0.0), axis=1, keepdims=True)


def gathered_row(column, eye):
    return jnp.sum(jnp.where(eye, column, 0.0), axis=0, keepdims=True)


def diagonal():
    shape = (128, 128)
    return lax.broadcasted_iota(jnp.int32, shape, 0) == lax.broadcasted_iota(jnp.int32, shape, 1)


def stat_rows(m, l):
    high = l.astype(jnp.bfloat16).astype(jnp.float32)
    return jnp.concatenate([m, high, l - high, jnp.zeros((5, 128), jnp.float32)], axis=0)


def prepare_kernel(info, k_ref, v_ref, vx, *masked):
    nkv, span = k_ref.shape[:2]
    me = tuple(info[i] for i in range(5))
    length, start = info[5], info[6]
    shard = (me[0] * 2 + me[1]) * 4 + me[2]
    lane = lax.broadcasted_iota(jnp.int32, (1, 128), 1)
    da = ((lane >> 5) & 1) | ((lane >> 3) & 2)
    seen = []
    for db in range(RING):
        z, yh, x = source(me, da, db, (lane >> 3) & 1)
        count = start + z * 64 + yh * 32 + x * 8 + (lane & 7) + 1 - shard * span
        seen.append(jnp.where(lane < 64, jnp.minimum(count, length), span))
    chunk = 256

    def fill(i, _):
        at = pl.ds(pl.multiple_of(i * chunk, chunk), chunk)
        slot = i * chunk + lax.broadcasted_iota(jnp.int32, (chunk, 128), 0)
        for count, kx in zip(seen, masked):
            mask = jnp.where(slot >= count, NEG, 0.0).astype(jnp.bfloat16)
            for kv in range(nkv):
                kx[kv, at, :128] = k_ref[kv, at, :]
                kx[kv, at, 128:] = mask
        for kv in range(nkv):
            vx[kv, at, :128] = v_ref[kv, at, :]
            vx[kv, at, 128:] = jnp.ones((chunk, 128), jnp.bfloat16)
        return 0

    lax.fori_loop(0, span // chunk, fill, 0)


def prepare(info, k, v):
    vmem = pl.BlockSpec(memory_space=pltpu.VMEM)
    count = 1 + RING
    return pl.pallas_call(
        prepare_kernel,
        in_specs=[pl.BlockSpec(memory_space=pltpu.SMEM), vmem, vmem],
        out_specs=[vmem] * count,
        out_shape=[jax.ShapeDtypeStruct((*k.shape[:2], 256), jnp.bfloat16)] * count,
        compiler_params=pltpu.CompilerParams(vmem_limit_bytes=4 * MIB),
        name="prepare",
    )(info, k, v)


def attend_kernel(q_ref, kx, vx, o_ref, *, kvs, first, nb, tile, scale):
    step = pl.program_id(0)
    span = vx.shape[1]
    eye = diagonal()

    def rows_of(b, count):
        row = lax.broadcasted_iota(jnp.int32, (count * 128, 128), 0)
        lane = lax.broadcasted_iota(jnp.int32, (count * 128, 128), 1)
        token = (first + step * nb + b + (row >> 7)) * 8 + ((row >> 4) & 7)
        hot = jnp.where(lane == token, 1.0, 0.0).astype(jnp.bfloat16)
        heads = [q_ref[pl.ds(b, count), :, kv * 16 : (kv + 1) * 16, :].reshape(count * 128, 128) for kv in kvs]
        return [jnp.concatenate([h, hot], axis=1) for h in heads]

    def scores(q, kv, t):
        return lax.dot_general(
            q, kx[kv, pl.ds(t, tile), :], (((1,), (1,)), ((), ())), preferred_element_type=jnp.float32
        )

    def point(m):
        return jnp.maximum(m * scale, 0.01 * NEG).astype(jnp.bfloat16).astype(jnp.float32)

    def put(b, r, results):
        stats = []
        for i, (m, acc) in enumerate(results):
            o_ref[b, i * 128 : (i + 1) * 128, :] = acc[r, :128].astype(jnp.bfloat16)
            stats.append(stat_rows(gathered_row(m[r], eye), gathered_row(acc[r, 128:], eye)))
        o_ref[b, len(results) * 128 :, :] = jnp.concatenate(stats, axis=0).astype(jnp.bfloat16)

    ok, results = [], []
    for q, kv in zip(rows_of(0, nb), kvs):
        s0 = scores(q, kv, 0)
        m = point(jnp.max(s0, axis=1, keepdims=True))
        p = []
        for t in range(0, span, tile):
            s = s0 if t == 0 else scores(q, kv, t)
            p.append(jnp.exp2(s * scale - m).astype(jnp.bfloat16))
        acc = jnp.dot(jnp.concatenate(p, axis=1), vx[kv], preferred_element_type=jnp.float32)
        ok.append(jnp.min(jnp.where(acc[:, 128:] < BIG, 1.0, 0.0)))
        results.append((m, acc))
    for b in range(nb):
        put(b, slice(b * 128, (b + 1) * 128), results)

    @pl.when(functools.reduce(jnp.minimum, ok) < 0.5)
    def _():
        def block(b, _):
            results = []
            for q, kv in zip(rows_of(b, 1), kvs):

                def top(n, m):
                    s = scores(q, kv, pl.multiple_of(n * tile, tile))
                    return jnp.maximum(m, jnp.max(s, axis=1, keepdims=True))

                m = point(lax.fori_loop(0, span // tile, top, jnp.full((128, 1), NEG, jnp.float32)))

                def add(n, acc):
                    t = pl.multiple_of(n * tile, tile)
                    p = jnp.exp2(scores(q, kv, t) * scale - m).astype(jnp.bfloat16)
                    return acc + jnp.dot(p, vx[kv, pl.ds(t, tile), :], preferred_element_type=jnp.float32)

                results.append((m, lax.fori_loop(0, span // tile, add, jnp.zeros((128, 256), jnp.float32))))
            put(b, slice(0, 128), results)
            return 0

        lax.fori_loop(0, nb, block, 0)


def attend(q, kx, vx, kvs, first=0, blocks=8, nb=None):
    span = vx.shape[1]
    nb, tile = nb or blocks, 256
    skip = first // nb
    vmem = pl.BlockSpec(memory_space=pltpu.VMEM)
    return pl.pallas_call(
        functools.partial(
            attend_kernel, kvs=kvs, first=first, nb=nb, tile=tile, scale=math.log2(math.e) / math.sqrt(128)
        ),
        grid=(blocks // nb,),
        in_specs=[pl.BlockSpec((nb, *q.shape[1:]), lambda i: (skip + i, 0, 0, 0)), vmem, vmem],
        out_specs=pl.BlockSpec((nb, len(kvs) * 136, 128), lambda i: (i, 0, 0)),
        out_shape=jax.ShapeDtypeStruct((blocks, len(kvs) * 136, 128), jnp.bfloat16),
        compiler_params=pltpu.CompilerParams(vmem_limit_bytes=20 * MIB, dimension_semantics=("arbitrary",)),
        cost_estimate=pl.CostEstimate(
            flops=8 * blocks * len(kvs) * 128 * span * 128,
            bytes_accessed=4 * MIB,
            transcendentals=blocks * len(kvs) * 128 * span,
        ),
        name="attend_plane",
    )(q, kx, vx)


def merged(parts, kv, nkv, eye):
    stats = [p[nkv * 128 :, :].astype(jnp.float32)[kv * 8 : kv * 8 + 8] for p in parts]
    m = functools.reduce(jnp.maximum, [s[0:1] for s in stats])
    total = jnp.zeros((1, 128), jnp.float32)
    out = jnp.zeros((128, 128), jnp.float32)
    for p, s in zip(parts, stats):
        factor = jnp.exp2(s[0:1] - m)
        total = total + factor * (s[1:2] + s[2:3])
        out = out + spread(factor, eye) * p[kv * 128 : (kv + 1) * 128, :].astype(jnp.float32)
    return out, m, total


def combine_kernel(*refs, starts):
    parts, o_ref = refs[:-1], refs[-1]
    nkv = o_ref.shape[1] // 136
    eye = diagonal()
    for b in range(o_ref.shape[0]):
        here = [part.at[at + b] for part, at in zip(parts, starts)]
        stats = []
        for kv in range(nkv):
            out, m, total = merged(here, kv, nkv, eye)
            o_ref[b, kv * 128 : (kv + 1) * 128, :] = out.astype(jnp.bfloat16)
            stats.append(stat_rows(m, total))
        o_ref[b, nkv * 128 :, :] = jnp.concatenate(stats, axis=0).astype(jnp.bfloat16)


def combine(blocks, *parts):
    vmem = pl.BlockSpec(memory_space=pltpu.VMEM)
    arrays, starts = zip(*parts)
    return pl.pallas_call(
        functools.partial(combine_kernel, starts=starts),
        in_specs=[vmem] * len(arrays),
        out_specs=vmem,
        out_shape=jax.ShapeDtypeStruct((blocks, *arrays[0].shape[1:]), jnp.bfloat16),
        compiler_params=pltpu.CompilerParams(vmem_limit_bytes=8 * MIB),
        name="combine",
    )(*arrays)


def finish_kernel(mine, theirs, o_ref, rows):
    eye = diagonal()
    nkv = mine.shape[1] // 136
    for kv in range(nkv):
        for dy in range(2):
            out, _, total = merged([mine.at[dy], theirs.at[1 - dy]], kv, nkv, eye)
            rows[kv, dy] = out * spread(1.0 / total, eye)
    for kv, h in itertools.product(range(nkv), range(16)):
        c = (kv * 16 + h) * 128
        both = [rows[kv, dy, pl.ds(h, 8, stride=16), :] for dy in range(2)]
        o_ref[:, c : c + 128] = jnp.concatenate(both, axis=0).astype(jnp.bfloat16)


def finish(mine, theirs):
    vmem = pl.BlockSpec(memory_space=pltpu.VMEM)
    nkv = mine.shape[1] // 136
    return pl.pallas_call(
        finish_kernel,
        in_specs=[vmem, vmem],
        out_specs=vmem,
        scratch_shapes=[pltpu.VMEM((nkv, 2, 128, 128), jnp.float32)],
        compiler_params=pltpu.CompilerParams(vmem_limit_bytes=4 * MIB),
        out_shape=jax.ShapeDtypeStruct((16, nkv * 2048), jnp.bfloat16),
        name="finish",
    )(mine, theirs)


def assemble_kernel(*refs, count):
    at = 0
    for x in refs[:count]:
        refs[-1][at : at + x.shape[0]] = x[...]
        at += x.shape[0]


def assemble(pieces, *others):
    vmem = pl.BlockSpec(memory_space=pltpu.VMEM)
    rows = sum(p.shape[0] for p in pieces)
    return pl.pallas_call(
        functools.partial(assemble_kernel, count=len(pieces)),
        in_specs=[vmem] * len(pieces) + [pl.BlockSpec(memory_space=pl.ANY)] * len(others),
        out_specs=vmem,
        out_shape=jax.ShapeDtypeStruct((rows, *pieces[0].shape[1:]), pieces[0].dtype),
        compiler_params=pltpu.CompilerParams(vmem_limit_bytes=4 * MIB),
        name="assemble",
    )(*pieces, *others)


def times_weight(halves, w_ref):
    x = jnp.concatenate([h[...] for h in halves], axis=0)
    return jnp.dot(x, w_ref[...], preferred_element_type=jnp.float32)


def project_kernel(xa, xb, w_ref, o_ref):
    o_ref[...] = times_weight((xa, xb), w_ref)


def project(xa, xb, w):
    vmem = pl.BlockSpec(memory_space=pltpu.VMEM)
    rows = xa.shape[0] + xb.shape[0]
    return pl.pallas_call(
        project_kernel,
        in_specs=[vmem] * 3,
        out_specs=vmem,
        out_shape=jax.ShapeDtypeStruct((rows, w.shape[1]), jnp.float32),
        compiler_params=pltpu.CompilerParams(vmem_limit_bytes=8 * MIB),
        cost_estimate=pl.CostEstimate(flops=2 * rows * w.shape[0] * w.shape[1], bytes_accessed=MIB, transcendentals=0),
        name="project",
    )(xa, xb, w)


def place_kernel(info, y0, y1, y3, xa, xb, w_ref, o_ref):
    me = tuple(info[i] for i in range(5))
    yl, core = me[3], me[4]
    y2 = times_weight((xa, xb), w_ref)
    for db, y in ((0, y0), (1, y1), (2, y2), (3, y3)):
        for da, dy in itertools.product(range(RING), range(2)):
            z, yh, xx = source(me, da, db, dy)
            row = (((z & 1) ^ core) * 2 + ((z >> 1) ^ yl)) * 64 + yh * 32 + xx * 8
            at = da * 16 + dy * 8
            o_ref[pl.ds(pl.multiple_of(row, 8), 8), :] = y[at : at + 8, :]


def place(info, y0, y1, y3, xa, xb, w):
    vmem = pl.BlockSpec(memory_space=pltpu.VMEM)
    return pl.pallas_call(
        place_kernel,
        in_specs=[pl.BlockSpec(memory_space=pltpu.SMEM)] + [vmem] * 6,
        out_specs=vmem,
        out_shape=jax.ShapeDtypeStruct((RING * y0.shape[0], w.shape[1]), jnp.float32),
        compiler_params=pltpu.CompilerParams(vmem_limit_bytes=8 * MIB),
        name="place",
    )(info, y0, y1, y3, xa, xb, w)


def on_device(queries, keys, values, lengths, start, out_weight):
    nkv = keys.shape[1]
    me = coords(lax.axis_index("cp"), lax.axis_index("tp"))
    info = jnp.concatenate([jnp.stack(me).astype(jnp.int32), lengths, start])
    k = keys.transpose(1, 0, 2)
    v = values.transpose(1, 0, 2)
    q = queries[None]
    q = jnp.concatenate([q, moved(q, yh=1)], axis=0)
    q, k, v, info = together(q, k, v, info)
    vx, kx0, kx1, kx2, kx3 = prepare(info, k, v)
    q2, q1, q3 = (moved(q, a=d) for d in (2, 1, 3))
    q2, vx, kx0, kx1, kx2, kx3 = together(q2, vx, kx0, kx1, kx2, kx3)
    q = assemble([q, q2, q1, q3], moved(q2, core=1))

    q2, q1, q3 = (moved(q, b=d) for d in (2, 1, 3))
    kvs = tuple(range(nkv))
    own = attend(q, kx0, vx, kvs, nb=4)
    q2, own = together(q2, own)
    p2 = attend(q2, kx2, vx, kvs)
    r2 = moved(p2, b=-2)
    q1, q3, p2 = together(q1, q3, p2)
    p1 = attend(q1, kx1, vx, kvs)
    r1 = moved(p1, b=-1)
    q3, p1 = together(q3, p1)
    p3a = attend(q3, kx3, vx, kvs, 0, 4)
    r3a = moved(p3a, b=-3)
    q3, p3a, r2 = together(q3, p3a, r2)
    p3b = attend(q3, kx3, vx, kvs, 4, 4)
    r3b = moved(p3b, b=-3)
    low = combine(4, (own, 0), (r1, 0), (r2, 0), (r3a, 0))
    s2 = moved(low[2:], a=-2)
    high = combine(4, (own, 4), (r1, 4), (r2, 4), (r3b, 0))
    s1, s3 = moved(high[:2], a=-1), moved(high[2:], a=-3)
    c = combine(2, (low, 0), (s1, 0), (s2, 0), (s3, 0))
    attn = finish(c, moved(c, yh=1))
    x2, x1, x3 = (moved(attn, a=d) for d in (2, 1, 3))
    low = assemble([attn, x1], moved(x2, core=1))
    high = assemble([x2, x3])
    x1a, x3b = moved(low, b=1), moved(high, b=3)
    x1b, x3a = moved(high, b=1), moved(low, b=3)
    x2a, x2b = moved(x1a, b=1), moved(x3b, b=3)
    ys = [project(xa, xb, out_weight) for xa, xb in ((low, high), (x1a, x1b), (x3a, x3b))]
    y = place(info, *ys, x2a, x2b, out_weight)
    y = y[:128] + moved(y[128:], core=1)
    y = y[:64] + moved(y[64:].astype(jnp.bfloat16), yl=1).astype(jnp.float32)
    return y.astype(jnp.bfloat16)


def solution(mesh):
    in_specs = (
        P("cp", "tp", None),
        P("cp", "tp", None),
        P("cp", "tp", None),
        P("cp"),
        P(),
        P("tp", "cp"),
    )
    return jax.shard_map(on_device, mesh=mesh, in_specs=in_specs, out_specs=P("tp", "cp"), check_vma=False)
```

profile of v0, /device:TPU:0, one launch (start us, length us, event | category | flops | bytes accessed | tf_op | source)
XLA Modules:
  0.0 106.0 jit_solution(17081744845200488099)
XLA Ops:
  0.0 3.3 %collective-permute-start = (bf16[1,8,32,128]{3,2,1,0:T(8,128)(2,1)}, bf16[1,8,32,128]{3,2,1,0:T(8,128)(2,1)S(1)}, u32[]{:S(2)}, u32[]{:S(2)}) collective-permute-start(bf16[1,8,32,128]{3,2,1,0:T(8,128)(2,1)} %bitcast.10), channel_id=1, source_target_pairs={{0,16},{1,17},{2,18},{3,19},{4,20},{5,21},{6,22},{7,23},{8,24},{9,... | collective-permute-start | bytes 196616 | tf_op jit(solution)/shard_map/ppermute | solution.py:32
  3.3 1.8 %copy_bitcast_fusion = (bf16[2,2048,128]{2,1,0:T(8,128)(2,1)S(1)}, bf16[2,2048,128]{2,1,0:T(8,128)(2,1)S(1)}) fusion(bf16[2048,2,128]{2,1,0:T(2,128)(2,1)} %param.8, bf16[2048,2,128]{2,1,0:T(2,128)(2,1)} %param.7), kind=kLoop, calls=%fused_computation | loop fusion | bytes 4194304 | tf_op jit(solution)/shard_map/transpose | solution.py:334
  6.6 4.0 %collective-permute-start.1 = (bf16[2,8,32,128]{3,2,1,0:T(8,128)(2,1)S(1)}, bf16[2,8,32,128]{3,2,1,0:T(8,128)(2,1)S(1)}, u32[]{:S(2)}, u32[]{:S(2)}) collective-permute-start(bf16[2,8,32,128]{3,2,1,0:T(8,128)(2,1)S(1)} %pad_maximum_fusion.refs_0_), channel_id=1, source_target_pairs={{0,64},{1,9},{2,66},{3,11},{4,68},{5,13},{6,70},{7,15},{8,72},{9,1... | collective-permute-start | bytes 393224 | tf_op jit(solution)/shard_map/ppermute | solution.py:32
  11.5 2.2 %collective-permute-start.3 = (bf16[2,8,32,128]{3,2,1,0:T(8,128)(2,1)S(1)}, bf16[2,8,32,128]{3,2,1,0:T(8,128)(2,1)S(1)}, u32[]{:S(2)}, u32[]{:S(2)}) collective-permute-start(bf16[2,8,32,128]{3,2,1,0:T(8,128)(2,1)S(1)} %pad_maximum_fusion.refs_0_), channel_id=1, source_target_pairs={{0,96},{1,13},{2,98},{3,15},{4,100},{5,1},{6,102},{7,3},{8,104},{9... | collective-permute-start | bytes 393224 | tf_op jit(solution)/shard_map/ppermute | solution.py:32
  13.8 2.0 %prepare.1 = (bf16[2,2048,256]{2,1,0:T(8,128)(2,1)S(1)}, bf16[2,2048,256]{2,1,0:T(8,128)(2,1)S(1)}, bf16[2,2048,256]{2,1,0:T(8,128)(2,1)S(1)}, bf16[2,2048,256]{...) custom-call(s32[7]{0:T(128)S(1)} %concatenate.7.info, bf16[2,2048,128]{2,1,0:T(8,128)(2,1)S(1)} %get-tuple-element.29.k_ref, ...), custom_call_target="tpu_custom_call" | custom-call | tf_op jit(solution)/shard_map/prepare/pallas_call | solution.py:97
  17.2 3.1 %collective-permute-start.5 = (bf16[8,8,32,128]{3,2,1,0:T(8,128)(2,1)S(1)}, bf16[8,8,32,128]{3,2,1,0:T(8,128)(2,1)S(1)}, u32[]{:S(2)}, u32[]{:S(2)}) collective-permute-start(bf16[8,8,32,128]{3,2,1,0:T(8,128)(2,1)S(1)} %assemble.3.q_ref), channel_id=1, source_target_pairs={{0,8},{1,65},{2,10},{3,67},{4,12},{5,69},{6,14},{7,71},{8,0},{9,73... | collective-permute-start | bytes 1572872 | tf_op jit(solution)/shard_map/ppermute | solution.py:32
  20.9 2.6 %collective-permute-start.7 = (bf16[8,8,32,128]{3,2,1,0:T(8,128)(2,1)S(1)}, bf16[8,8,32,128]{3,2,1,0:T(8,128)(2,1)S(1)}, u32[]{:S(2)}, u32[]{:S(2)}) collective-permute-start(bf16[8,8,32,128]{3,2,1,0:T(8,128)(2,1)S(1)} %assemble.3.q_ref), channel_id=1, source_target_pairs={{0,12},{1,97},{2,14},{3,99},{4,0},{5,101},{6,2},{7,103},{8,4},{9,1... | collective-permute-start | bytes 1572872 | tf_op jit(solution)/shard_map/ppermute | solution.py:32
  23.6 5.5 %attend_plane.5.refs_0_ = bf16[8,272,128]{2,1,0:T(8,128)(2,1)S(1)} custom-call(bf16[8,8,32,128]{3,2,1,0:T(8,128)(2,1)S(1)} %assemble.3.q_ref, bf16[2,2048,256]{2,1,0:T(8,128)(2,1)S(1)} %get-tuple-element.37.kx, bf16[2,2048,256]{2,1,0:T(8,128)(2,1)S(1)} %get-tuple-element.38.vx), custom_call_target="tpu_custom_call" | custom-call | flops 4294967296 | bytes 4194304 | tf_op jit(solution)/shard_map/attend_plane/pallas_call | solution.py:178
  29.1 4.9 %attend_plane.6 = bf16[8,272,128]{2,1,0:T(8,128)(2,1)S(1)} custom-call(bf16[8,8,32,128]{3,2,1,0:T(8,128)(2,1)S(1)} %collective-permute-done.5.q_ref, bf16[2,2048,256]{2,1,0:T(8,128)(2,1)S(1)} %get-tuple-element.41.kx, bf16[2,2048,256]{2,1,0:T(8,128)(2,1)S(1)} %get-tuple-element.38.vx), custom_call_target="tpu_custom_call" | custom-call | flops 4294967296 | bytes 4194304 | tf_op jit(solution)/shard_map/attend_plane/pallas_call | solution.py:178
  34.1 2.3 %collective-permute-start.9 = (bf16[8,272,128]{2,1,0:T(8,128)(2,1)S(1)}, bf16[8,272,128]{2,1,0:T(8,128)(2,1)S(1)}, u32[]{:S(2)}, u32[]{:S(2)}) collective-permute-start(bf16[8,272,128]{2,1,0:T(8,128)(2,1)S(1)} %attend_plane.6), channel_id=1, source_target_pairs={{0,8},{1,65},{2,10},{3,67},{4,12},{5,69},{6,14},{7,71},{8,0},{9,73... | collective-permute-start | bytes 1671176 | tf_op jit(solution)/shard_map/ppermute | solution.py:32
  36.3 4.9 %attend_plane.7 = bf16[8,272,128]{2,1,0:T(8,128)(2,1)S(1)} custom-call(bf16[8,8,32,128]{3,2,1,0:T(8,128)(2,1)S(1)} %collective-permute-done.6.q_ref, bf16[2,2048,256]{2,1,0:T(8,128)(2,1)S(1)} %get-tuple-element.43.kx, bf16[2,2048,256]{2,1,0:T(8,128)(2,1)S(1)} %get-tuple-element.38.vx), custom_call_target="tpu_custom_call" | custom-call | flops 4294967296 | bytes 4194304 | tf_op jit(solution)/shard_map/attend_plane/pallas_call | solution.py:178
  41.3 1.2 %collective-permute-start.8 = (bf16[8,272,128]{2,1,0:T(8,128)(2,1)S(1)}, bf16[8,272,128]{2,1,0:T(8,128)(2,1)S(1)}, u32[]{:S(2)}, u32[]{:S(2)}) collective-permute-start(bf16[8,272,128]{2,1,0:T(8,128)(2,1)S(1)} %attend_plane.7), channel_id=1, source_target_pairs={{0,12},{1,97},{2,14},{3,99},{4,0},{5,101},{6,2},{7,103},{8,4},{9,1... | collective-permute-start | bytes 1671176 | tf_op jit(solution)/shard_map/ppermute | solution.py:32
  42.5 2.8 %attend_plane.8 = bf16[4,272,128]{2,1,0:T(8,128)(2,1)S(1)} custom-call(bf16[8,8,32,128]{3,2,1,0:T(8,128)(2,1)S(1)} %collective-permute-done.7.q_ref, bf16[2,2048,256]{2,1,0:T(8,128)(2,1)S(1)} %get-tuple-element.46.kx, bf16[2,2048,256]{2,1,0:T(8,128)(2,1)S(1)} %get-tuple-element.38.vx), custom_call_target="tpu_custom_call" | custom-call | flops 2147483648 | bytes 4194304 | tf_op jit(solution)/shard_map/attend_plane/pallas_call | solution.py:178
  46.2 3.0 %attend_plane.9 = bf16[4,272,128]{2,1,0:T(8,128)(2,1)S(1)} custom-call(bf16[8,8,32,128]{3,2,1,0:T(8,128)(2,1)S(1)} %collective-permute-done.7.q_ref, bf16[2,2048,256]{2,1,0:T(8,128)(2,1)S(1)} %get-tuple-element.46.kx, bf16[2,2048,256]{2,1,0:T(8,128)(2,1)S(1)} %get-tuple-element.38.vx), custom_call_target="tpu_custom_call" | custom-call | flops 2147483648 | bytes 4194304 | tf_op jit(solution)/shard_map/attend_plane/pallas_call | solution.py:178
  49.9 3.2 %collective-permute-done.10.refs_3_ = bf16[4,272,128]{2,1,0:T(8,128)(2,1)S(1)} collective-permute-done((bf16[4,272,128]{2,1,0:T(8,128)(2,1)S(1)}, bf16[4,272,128]{2,1,0:T(8,128)(2,1)S(1)}, u32[]{:S(2)}, u32[]{:S(2)}) %collective-permute-start.10) | collective-permute-done | bytes 278560 | tf_op jit(solution)/shard_map/ppermute | solution.py:32
  53.8 1.4 %collective-permute-start.13 = (bf16[2,272,128]{2,1,0:T(8,128)(2,1)S(1)}, bf16[2,272,128]{2,1,0:T(8,128)(2,1)S(1)}, u32[]{:S(2)}, u32[]{:S(2)}) collective-permute-start(bf16[2,272,128]{2,1,0:T(8,128)(2,1)S(1)} %slice.30), channel_id=1, source_target_pairs={{0,64},{1,9},{2,66},{3,11},{4,68},{5,13},{6,70},{7,15},{8,72},{9,1... | collective-permute-start | bytes 417800 | tf_op jit(solution)/shard_map/ppermute | solution.py:32
  55.1 3.1 %collective-permute-done.11.refs_3_ = bf16[4,272,128]{2,1,0:T(8,128)(2,1)S(1)} collective-permute-done((bf16[4,272,128]{2,1,0:T(8,128)(2,1)S(1)}, bf16[4,272,128]{2,1,0:T(8,128)(2,1)S(1)}, u32[]{:S(2)}, u32[]{:S(2)}) %collective-permute-start.11) | collective-permute-done | bytes 278560 | tf_op jit(solution)/shard_map/ppermute | solution.py:32
  59.0 2.1 %collective-permute-start.12 = (bf16[2,272,128]{2,1,0:T(8,128)(2,1)S(1)}, bf16[2,272,128]{2,1,0:T(8,128)(2,1)S(1)}, u32[]{:S(2)}, u32[]{:S(2)}) collective-permute-start(bf16[2,272,128]{2,1,0:T(8,128)(2,1)S(1)} %get-tuple-element.50), channel_id=1, source_target_pairs={{0,96},{1,13},{2,98},{3,15},{4,100},{5,1},{6,102},{7,3},{8,104},{9... | collective-permute-start | bytes 417800 | tf_op jit(solution)/shard_map/ppermute | solution.py:32
  61.1 3.0 %collective-permute-done.12.refs_1_ = bf16[2,272,128]{2,1,0:T(8,128)(2,1)S(1)} collective-permute-done((bf16[2,272,128]{2,1,0:T(8,128)(2,1)S(1)}, bf16[2,272,128]{2,1,0:T(8,128)(2,1)S(1)}, u32[]{:S(2)}, u32[]{:S(2)}) %collective-permute-start.12) | collective-permute-done | bytes 139296 | tf_op jit(solution)/shard_map/ppermute | solution.py:32
  64.1 3.2 %collective-permute-done.14.refs_3_ = bf16[2,272,128]{2,1,0:T(8,128)(2,1)S(1)} collective-permute-done((bf16[2,272,128]{2,1,0:T(8,128)(2,1)S(1)}, bf16[2,272,128]{2,1,0:T(8,128)(2,1)S(1)}, u32[]{:S(2)}, u32[]{:S(2)}) %collective-permute-start.14) | collective-permute-done | bytes 139296 | tf_op jit(solution)/shard_map/ppermute | solution.py:32
  67.7 2.8 %collective-permute-start.15 = (bf16[2,272,128]{2,1,0:T(8,128)(2,1)S(1)}, bf16[2,272,128]{2,1,0:T(8,128)(2,1)S(1)}, u32[]{:S(2)}, u32[]{:S(2)}) collective-permute-start(bf16[2,272,128]{2,1,0:T(8,128)(2,1)S(1)} %combine.5.mine), channel_id=1, source_target_pairs={{0,16},{1,17},{2,18},{3,19},{4,20},{5,21},{6,22},{7,23},{8,24},{9,... | collective-permute-start | bytes 417800 | tf_op jit(solution)/shard_map/ppermute | solution.py:32
  70.5 3.8 %collective-permute-done.15.theirs = bf16[2,272,128]{2,1,0:T(8,128)(2,1)S(1)} collective-permute-done((bf16[2,272,128]{2,1,0:T(8,128)(2,1)S(1)}, bf16[2,272,128]{2,1,0:T(8,128)(2,1)S(1)}, u32[]{:S(2)}, u32[]{:S(2)}) %collective-permute-start.15) | collective-permute-done | bytes 139296 | tf_op jit(solution)/shard_map/ppermute | solution.py:32
  74.8 1.5 %collective-permute-start.19 = (bf16[16,4096]{1,0:T(8,128)(2,1)S(1)}, bf16[16,4096]{1,0:T(8,128)(2,1)S(1)}, u32[]{:S(2)}, u32[]{:S(2)}) collective-permute-start(bf16[16,4096]{1,0:T(8,128)(2,1)S(1)} %finish.1.refs_0_), channel_id=1, source_target_pairs={{0,96},{1,13},{2,98},{3,15},{4,100},{5,1},{6,102},{7,3},{8,104},{9... | collective-permute-start | bytes 393224 | tf_op jit(solution)/shard_map/ppermute | solution.py:32
  76.9 4.4 %collective-permute-done.17.refs_0_ = bf16[16,4096]{1,0:T(8,128)(2,1)S(1)} collective-permute-done((bf16[16,4096]{1,0:T(8,128)(2,1)S(1)}, bf16[16,4096]{1,0:T(8,128)(2,1)S(1)}, u32[]{:S(2)}, u32[]{:S(2)}) %collective-permute-start.17) | collective-permute-done | bytes 131104 | tf_op jit(solution)/shard_map/ppermute | solution.py:32
  83.5 2.5 %collective-permute-start.22 = (bf16[32,4096]{1,0:T(8,128)(2,1)S(1)}, bf16[32,4096]{1,0:T(8,128)(2,1)S(1)}, u32[]{:S(2)}, u32[]{:S(2)}) collective-permute-start(bf16[32,4096]{1,0:T(8,128)(2,1)S(1)} %assemble.4.xa), channel_id=1, source_target_pairs={{0,12},{1,97},{2,14},{3,99},{4,0},{5,101},{6,2},{7,103},{8,4},{9,1... | collective-permute-start | bytes 786440 | tf_op jit(solution)/shard_map/ppermute | solution.py:32
  86.0 1.8 %collective-permute-done.23.xb = bf16[32,4096]{1,0:T(8,128)(2,1)S(1)} collective-permute-done((bf16[32,4096]{1,0:T(8,128)(2,1)S(1)}, bf16[32,4096]{1,0:T(8,128)(2,1)S(1)}, u32[]{:S(2)}, u32[]{:S(2)}) %collective-permute-start.23) | collective-permute-done | bytes 262176 | tf_op jit(solution)/shard_map/ppermute | solution.py:32
  87.7 2.3 %collective-permute-start.25 = (bf16[32,4096]{1,0:T(8,128)(2,1)S(1)}, bf16[32,4096]{1,0:T(8,128)(2,1)S(1)}, u32[]{:S(2)}, u32[]{:S(2)}) collective-permute-start(bf16[32,4096]{1,0:T(8,128)(2,1)S(1)} %collective-permute-done.23.xb), channel_id=1, source_target_pairs={{0,12},{1,97},{2,14},{3,99},{4,0},{5,101},{6,2},{7,103},{8,4},{9,1... | collective-permute-start | bytes 786440 | tf_op jit(solution)/shard_map/ppermute | solution.py:32
  92.1 1.5 %collective-permute-done.21.xb = bf16[32,4096]{1,0:T(8,128)(2,1)S(1)} collective-permute-done((bf16[32,4096]{1,0:T(8,128)(2,1)S(1)}, bf16[32,4096]{1,0:T(8,128)(2,1)S(1)}, u32[]{:S(2)}, u32[]{:S(2)}) %collective-permute-start.21) | collective-permute-done | bytes 262176 | tf_op jit(solution)/shard_map/ppermute | solution.py:32
  94.4 3.5 %collective-permute-done.24.xa = bf16[32,4096]{1,0:T(8,128)(2,1)S(1)} collective-permute-done((bf16[32,4096]{1,0:T(8,128)(2,1)S(1)}, bf16[32,4096]{1,0:T(8,128)(2,1)S(1)}, u32[]{:S(2)}, u32[]{:S(2)}) %collective-permute-start.24) | collective-permute-done | bytes 262176 | tf_op jit(solution)/shard_map/ppermute | solution.py:32
  97.9 1.4 %place.1 = f32[256,512]{1,0:T(8,128)S(1)} custom-call(s32[7]{0:T(128)S(1)} %concatenate.7.info, f32[64,512]{1,0:T(8,128)S(1)} %project.3.y0, f32[64,512]{1,0:T(8,128)S(1)} %project.4.y1, f32[64,512]{1,0:T(8,128)S(1)} %project.5.y3, bf16[32,4096]{1,0:T(8,128)(2,1)S(1)} %collective-permute-done.24.xa, bf16[32,4096]{1,0:T(8,128)(2,1)S(1)} %collective-permute-done.25.xb, ...), custom_call_target="tpu_custom_call" | custom-call | tf_op jit(solution)/shard_map/place/pallas_call | solution.py:319
  99.4 1.5 %collective-permute-done.26 = f32[128,512]{1,0:T(8,128)S(1)} collective-permute-done((f32[128,512]{1,0:T(8,128)S(1)}, f32[128,512]{1,0:T(8,128)S(1)}, u32[]{:S(2)}, u32[]{:S(2)}) %collective-permute-start.26) | collective-permute-done | bytes 262176 | tf_op jit(solution)/shard_map/ppermute | solution.py:32
  102.2 3.2 %collective-permute-done.27 = bf16[64,512]{1,0:T(8,128)(2,1)S(1)} collective-permute-done((bf16[64,512]{1,0:T(8,128)(2,1)S(1)}, bf16[64,512]{1,0:T(8,128)(2,1)S(1)}, u32[]{:S(2)}, u32[]{:S(2)}) %collective-permute-start.27) | collective-permute-done | bytes 65568 | tf_op jit(solution)/shard_map/ppermute | solution.py:32
  (54 shorter events, 14.6 us)
Async XLA Ops:
  0.0 6.5 %copy-start.1 = (bf16[8,32,128]{2,1,0:T(8,128)(2,1)S(1)}, bf16[8,32,128]{2,1,0:T(8,128)(2,1)}, u32[]{:S(2)}) copy-start(bf16[8,32,128]{2,1,0:T(8,128)(2,1)} %param.6) | copy-start | bytes 196612
  0.0 6.5 %collective-permute-start = (bf16[1,8,32,128]{3,2,1,0:T(8,128)(2,1)}, bf16[1,8,32,128]{3,2,1,0:T(8,128)(2,1)S(1)}, u32[]{:S(2)}, u32[]{:S(2)}) collective-permute-start(bf16[1,8,32,128]{3,2,1,0:T(8,128)(2,1)} %bitcast.10), channel_id=1, source_target_pairs={{0,16},{1,17},{2,18},{3,19},{4,20},{5,21},{6,22},{7,23},{8,24},{9,... | collective-permute-start | bytes 196616 | tf_op jit(solution)/shard_map/ppermute | solution.py:32
  6.6 9.2 %collective-permute-start.1 = (bf16[2,8,32,128]{3,2,1,0:T(8,128)(2,1)S(1)}, bf16[2,8,32,128]{3,2,1,0:T(8,128)(2,1)S(1)}, u32[]{:S(2)}, u32[]{:S(2)}) collective-permute-start(bf16[2,8,32,128]{3,2,1,0:T(8,128)(2,1)S(1)} %pad_maximum_fusion.refs_0_), channel_id=1, source_target_pairs={{0,64},{1,9},{2,66},{3,11},{4,68},{5,13},{6,70},{7,15},{8,72},{9,1... | collective-permute-start | bytes 393224 | tf_op jit(solution)/shard_map/ppermute | solution.py:32
  10.5 6.2 %collective-permute-start.2 = (bf16[2,8,32,128]{3,2,1,0:T(8,128)(2,1)S(1)}, bf16[2,8,32,128]{3,2,1,0:T(8,128)(2,1)S(1)}, u32[]{:S(2)}, u32[]{:S(2)}) collective-permute-start(bf16[2,8,32,128]{3,2,1,0:T(8,128)(2,1)S(1)} %pad_maximum_fusion.refs_0_), channel_id=1, source_target_pairs={{0,32},{1,5},{2,34},{3,7},{4,36},{5,9},{6,38},{7,11},{8,40},{9,13}... | collective-permute-start | bytes 393224 | tf_op jit(solution)/shard_map/ppermute | solution.py:32
  11.5 5.2 %collective-permute-start.3 = (bf16[2,8,32,128]{3,2,1,0:T(8,128)(2,1)S(1)}, bf16[2,8,32,128]{3,2,1,0:T(8,128)(2,1)S(1)}, u32[]{:S(2)}, u32[]{:S(2)}) collective-permute-start(bf16[2,8,32,128]{3,2,1,0:T(8,128)(2,1)S(1)} %pad_maximum_fusion.refs_0_), channel_id=1, source_target_pairs={{0,96},{1,13},{2,98},{3,15},{4,100},{5,1},{6,102},{7,3},{8,104},{9... | collective-permute-start | bytes 393224 | tf_op jit(solution)/shard_map/ppermute | solution.py:32
  15.7 1.4 %collective-permute-start.4 = (bf16[2,8,32,128]{3,2,1,0:T(8,128)(2,1)S(1)}, bf16[2,8,32,128]{3,2,1,0:T(8,128)(2,1)S(1)}, u32[]{:S(2)}, u32[]{:S(2)}) collective-permute-start(bf16[2,8,32,128]{3,2,1,0:T(8,128)(2,1)S(1)} %collective-permute-done.1.refs_1_), channel_id=1, source_target_pairs={{0,1},{1,0},{2,3},{3,2},{4,5},{5,4},{6,7},{7,6},{8,9},{9,8},{10,11... | collective-permute-start | bytes 393224 | tf_op jit(solution)/shard_map/ppermute | solution.py:32
  17.2 11.9 %collective-permute-start.5 = (bf16[8,8,32,128]{3,2,1,0:T(8,128)(2,1)S(1)}, bf16[8,8,32,128]{3,2,1,0:T(8,128)(2,1)S(1)}, u32[]{:S(2)}, u32[]{:S(2)}) collective-permute-start(bf16[8,8,32,128]{3,2,1,0:T(8,128)(2,1)S(1)} %assemble.3.q_ref), channel_id=1, source_target_pairs={{0,8},{1,65},{2,10},{3,67},{4,12},{5,69},{6,14},{7,71},{8,0},{9,73... | collective-permute-start | bytes 1572872 | tf_op jit(solution)/shard_map/ppermute | solution.py:32
  20.3 16.0 %collective-permute-start.6 = (bf16[8,8,32,128]{3,2,1,0:T(8,128)(2,1)S(1)}, bf16[8,8,32,128]{3,2,1,0:T(8,128)(2,1)S(1)}, u32[]{:S(2)}, u32[]{:S(2)}) collective-permute-start(bf16[8,8,32,128]{3,2,1,0:T(8,128)(2,1)S(1)} %assemble.3.q_ref), channel_id=1, source_target_pairs={{0,4},{1,33},{2,6},{3,35},{4,8},{5,37},{6,10},{7,39},{8,12},{9,41}... | collective-permute-start | bytes 1572872 | tf_op jit(solution)/shard_map/ppermute | solution.py:32
  20.9 15.4 %collective-permute-start.7 = (bf16[8,8,32,128]{3,2,1,0:T(8,128)(2,1)S(1)}, bf16[8,8,32,128]{3,2,1,0:T(8,128)(2,1)S(1)}, u32[]{:S(2)}, u32[]{:S(2)}) collective-permute-start(bf16[8,8,32,128]{3,2,1,0:T(8,128)(2,1)S(1)} %assemble.3.q_ref), channel_id=1, source_target_pairs={{0,12},{1,97},{2,14},{3,99},{4,0},{5,101},{6,2},{7,103},{8,4},{9,1... | collective-permute-start | bytes 1572872 | tf_op jit(solution)/shard_map/ppermute | solution.py:32
  34.1 12.1 %collective-permute-start.9 = (bf16[8,272,128]{2,1,0:T(8,128)(2,1)S(1)}, bf16[8,272,128]{2,1,0:T(8,128)(2,1)S(1)}, u32[]{:S(2)}, u32[]{:S(2)}) collective-permute-start(bf16[8,272,128]{2,1,0:T(8,128)(2,1)S(1)} %attend_plane.6), channel_id=1, source_target_pairs={{0,8},{1,65},{2,10},{3,67},{4,12},{5,69},{6,14},{7,71},{8,0},{9,73... | collective-permute-start | bytes 1671176 | tf_op jit(solution)/shard_map/ppermute | solution.py:32
  41.3 11.8 %collective-permute-start.8 = (bf16[8,272,128]{2,1,0:T(8,128)(2,1)S(1)}, bf16[8,272,128]{2,1,0:T(8,128)(2,1)S(1)}, u32[]{:S(2)}, u32[]{:S(2)}) collective-permute-start(bf16[8,272,128]{2,1,0:T(8,128)(2,1)S(1)} %attend_plane.7), channel_id=1, source_target_pairs={{0,12},{1,97},{2,14},{3,99},{4,0},{5,101},{6,2},{7,103},{8,4},{9,1... | collective-permute-start | bytes 1671176 | tf_op jit(solution)/shard_map/ppermute | solution.py:32
  45.2 7.8 %collective-permute-start.10 = (bf16[4,272,128]{2,1,0:T(8,128)(2,1)S(1)}, bf16[4,272,128]{2,1,0:T(8,128)(2,1)S(1)}, u32[]{:S(2)}, u32[]{:S(2)}) collective-permute-start(bf16[4,272,128]{2,1,0:T(8,128)(2,1)S(1)} %attend_plane.8), channel_id=1, source_target_pairs={{0,4},{1,33},{2,6},{3,35},{4,8},{5,37},{6,10},{7,39},{8,12},{9,41}... | collective-permute-start | bytes 835592 | tf_op jit(solution)/shard_map/ppermute | solution.py:32
  49.2 9.1 %collective-permute-start.11 = (bf16[4,272,128]{2,1,0:T(8,128)(2,1)S(1)}, bf16[4,272,128]{2,1,0:T(8,128)(2,1)S(1)}, u32[]{:S(2)}, u32[]{:S(2)}) collective-permute-start(bf16[4,272,128]{2,1,0:T(8,128)(2,1)S(1)} %attend_plane.9), channel_id=1, source_target_pairs={{0,4},{1,33},{2,6},{3,35},{4,8},{5,37},{6,10},{7,39},{8,12},{9,41}... | collective-permute-start | bytes 835592 | tf_op jit(solution)/shard_map/ppermute | solution.py:32
  53.8 36.6 %copy-start = (bf16[4096,512]{1,0:T(8,128)(2,1)S(1)}, bf16[4096,512]{1,0:T(8,128)(2,1)}, u32[]{:S(2)}) copy-start(bf16[4096,512]{1,0:T(8,128)(2,1)} %w_ref.7) | copy-start | bytes 12582916
  53.8 7.3 %collective-permute-start.13 = (bf16[2,272,128]{2,1,0:T(8,128)(2,1)S(1)}, bf16[2,272,128]{2,1,0:T(8,128)(2,1)S(1)}, u32[]{:S(2)}, u32[]{:S(2)}) collective-permute-start(bf16[2,272,128]{2,1,0:T(8,128)(2,1)S(1)} %slice.30), channel_id=1, source_target_pairs={{0,64},{1,9},{2,66},{3,11},{4,68},{5,13},{6,70},{7,15},{8,72},{9,1... | collective-permute-start | bytes 417800 | tf_op jit(solution)/shard_map/ppermute | solution.py:32
  59.0 5.1 %collective-permute-start.12 = (bf16[2,272,128]{2,1,0:T(8,128)(2,1)S(1)}, bf16[2,272,128]{2,1,0:T(8,128)(2,1)S(1)}, u32[]{:S(2)}, u32[]{:S(2)}) collective-permute-start(bf16[2,272,128]{2,1,0:T(8,128)(2,1)S(1)} %get-tuple-element.50), channel_id=1, source_target_pairs={{0,96},{1,13},{2,98},{3,15},{4,100},{5,1},{6,102},{7,3},{8,104},{9... | collective-permute-start | bytes 417800 | tf_op jit(solution)/shard_map/ppermute | solution.py:32
  61.1 6.3 %collective-permute-start.14 = (bf16[2,272,128]{2,1,0:T(8,128)(2,1)S(1)}, bf16[2,272,128]{2,1,0:T(8,128)(2,1)S(1)}, u32[]{:S(2)}, u32[]{:S(2)}) collective-permute-start(bf16[2,272,128]{2,1,0:T(8,128)(2,1)S(1)} %get-tuple-element.49), channel_id=1, source_target_pairs={{0,32},{1,5},{2,34},{3,7},{4,36},{5,9},{6,38},{7,11},{8,40},{9,13}... | collective-permute-start | bytes 417800 | tf_op jit(solution)/shard_map/ppermute | solution.py:32
  67.7 6.6 %collective-permute-start.15 = (bf16[2,272,128]{2,1,0:T(8,128)(2,1)S(1)}, bf16[2,272,128]{2,1,0:T(8,128)(2,1)S(1)}, u32[]{:S(2)}, u32[]{:S(2)}) collective-permute-start(bf16[2,272,128]{2,1,0:T(8,128)(2,1)S(1)} %combine.5.mine), channel_id=1, source_target_pairs={{0,16},{1,17},{2,18},{3,19},{4,20},{5,21},{6,22},{7,23},{8,24},{9,... | collective-permute-start | bytes 417800 | tf_op jit(solution)/shard_map/ppermute | solution.py:32
  74.7 6.6 %collective-permute-start.17 = (bf16[16,4096]{1,0:T(8,128)(2,1)S(1)}, bf16[16,4096]{1,0:T(8,128)(2,1)S(1)}, u32[]{:S(2)}, u32[]{:S(2)}) collective-permute-start(bf16[16,4096]{1,0:T(8,128)(2,1)S(1)} %finish.1.refs_0_), channel_id=1, source_target_pairs={{0,64},{1,9},{2,66},{3,11},{4,68},{5,13},{6,70},{7,15},{8,72},{9,1... | collective-permute-start | bytes 393224 | tf_op jit(solution)/shard_map/ppermute | solution.py:32
  74.8 6.5 %collective-permute-start.19 = (bf16[16,4096]{1,0:T(8,128)(2,1)S(1)}, bf16[16,4096]{1,0:T(8,128)(2,1)S(1)}, u32[]{:S(2)}, u32[]{:S(2)}) collective-permute-start(bf16[16,4096]{1,0:T(8,128)(2,1)S(1)} %finish.1.refs_0_), channel_id=1, source_target_pairs={{0,96},{1,13},{2,98},{3,15},{4,100},{5,1},{6,102},{7,3},{8,104},{9... | collective-permute-start | bytes 393224 | tf_op jit(solution)/shard_map/ppermute | solution.py:32
  76.2 6.4 %collective-permute-start.16 = (bf16[16,4096]{1,0:T(8,128)(2,1)S(1)}, bf16[16,4096]{1,0:T(8,128)(2,1)S(1)}, u32[]{:S(2)}, u32[]{:S(2)}) collective-permute-start(bf16[16,4096]{1,0:T(8,128)(2,1)S(1)} %finish.1.refs_0_), channel_id=1, source_target_pairs={{0,32},{1,5},{2,34},{3,7},{4,36},{5,9},{6,38},{7,11},{8,40},{9,13}... | collective-permute-start | bytes 393224 | tf_op jit(solution)/shard_map/ppermute | solution.py:32
  81.3 1.4 %collective-permute-start.18 = (bf16[16,4096]{1,0:T(8,128)(2,1)S(1)}, bf16[16,4096]{1,0:T(8,128)(2,1)S(1)}, u32[]{:S(2)}, u32[]{:S(2)}) collective-permute-start(bf16[16,4096]{1,0:T(8,128)(2,1)S(1)} %collective-permute-done.17.refs_0_), channel_id=1, source_target_pairs={{0,1},{1,0},{2,3},{3,2},{4,5},{5,4},{6,7},{7,6},{8,9},{9,8},{10,11... | collective-permute-start | bytes 393224 | tf_op jit(solution)/shard_map/ppermute | solution.py:32
  81.3 6.4 %collective-permute-start.23 = (bf16[32,4096]{1,0:T(8,128)(2,1)S(1)}, bf16[32,4096]{1,0:T(8,128)(2,1)S(1)}, u32[]{:S(2)}, u32[]{:S(2)}) collective-permute-start(bf16[32,4096]{1,0:T(8,128)(2,1)S(1)} %assemble.5.xb), channel_id=1, source_target_pairs={{0,12},{1,97},{2,14},{3,99},{4,0},{5,101},{6,2},{7,103},{8,4},{9,1... | collective-permute-start | bytes 786440 | tf_op jit(solution)/shard_map/ppermute | solution.py:32
  82.7 7.7 %collective-permute-start.20 = (bf16[32,4096]{1,0:T(8,128)(2,1)S(1)}, bf16[32,4096]{1,0:T(8,128)(2,1)S(1)}, u32[]{:S(2)}, u32[]{:S(2)}) collective-permute-start(bf16[32,4096]{1,0:T(8,128)(2,1)S(1)} %assemble.4.xa), channel_id=1, source_target_pairs={{0,4},{1,33},{2,6},{3,35},{4,8},{5,37},{6,10},{7,39},{8,12},{9,41}... | collective-permute-start | bytes 786440 | tf_op jit(solution)/shard_map/ppermute | solution.py:32
  83.5 7.7 %collective-permute-start.22 = (bf16[32,4096]{1,0:T(8,128)(2,1)S(1)}, bf16[32,4096]{1,0:T(8,128)(2,1)S(1)}, u32[]{:S(2)}, u32[]{:S(2)}) collective-permute-start(bf16[32,4096]{1,0:T(8,128)(2,1)S(1)} %assemble.4.xa), channel_id=1, source_target_pairs={{0,12},{1,97},{2,14},{3,99},{4,0},{5,101},{6,2},{7,103},{8,4},{9,1... | collective-permute-start | bytes 786440 | tf_op jit(solution)/shard_map/ppermute | solution.py:32
  86.0 7.6 %collective-permute-start.21 = (bf16[32,4096]{1,0:T(8,128)(2,1)S(1)}, bf16[32,4096]{1,0:T(8,128)(2,1)S(1)}, u32[]{:S(2)}, u32[]{:S(2)}) collective-permute-start(bf16[32,4096]{1,0:T(8,128)(2,1)S(1)} %assemble.5.xb), channel_id=1, source_target_pairs={{0,4},{1,33},{2,6},{3,35},{4,8},{5,37},{6,10},{7,39},{8,12},{9,41}... | collective-permute-start | bytes 786440 | tf_op jit(solution)/shard_map/ppermute | solution.py:32
  87.7 6.7 %collective-permute-start.25 = (bf16[32,4096]{1,0:T(8,128)(2,1)S(1)}, bf16[32,4096]{1,0:T(8,128)(2,1)S(1)}, u32[]{:S(2)}, u32[]{:S(2)}) collective-permute-start(bf16[32,4096]{1,0:T(8,128)(2,1)S(1)} %collective-permute-done.23.xb), channel_id=1, source_target_pairs={{0,12},{1,97},{2,14},{3,99},{4,0},{5,101},{6,2},{7,103},{8,4},{9,1... | collective-permute-start | bytes 786440 | tf_op jit(solution)/shard_map/ppermute | solution.py:32
  90.3 7.6 %collective-permute-start.24 = (bf16[32,4096]{1,0:T(8,128)(2,1)S(1)}, bf16[32,4096]{1,0:T(8,128)(2,1)S(1)}, u32[]{:S(2)}, u32[]{:S(2)}) collective-permute-start(bf16[32,4096]{1,0:T(8,128)(2,1)S(1)} %collective-permute-done.20.xa), channel_id=1, source_target_pairs={{0,4},{1,33},{2,6},{3,35},{4,8},{5,37},{6,10},{7,39},{8,12},{9,41}... | collective-permute-start | bytes 786440 | tf_op jit(solution)/shard_map/ppermute | solution.py:32
  99.3 1.6 %collective-permute-start.26 = (f32[128,512]{1,0:T(8,128)S(1)}, f32[128,512]{1,0:T(8,128)S(1)}, u32[]{:S(2)}, u32[]{:S(2)}) collective-permute-start(f32[128,512]{1,0:T(8,128)S(1)} %slice.33), channel_id=1, source_target_pairs={{0,1},{1,0},{2,3},{3,2},{4,5},{5,4},{6,7},{7,6},{8,9},{9,8},{10,11... | collective-permute-start | bytes 786440 | tf_op jit(solution)/shard_map/ppermute | solution.py:32
  101.0 4.3 %collective-permute-start.27 = (bf16[64,512]{1,0:T(8,128)(2,1)S(1)}, bf16[64,512]{1,0:T(8,128)(2,1)S(1)}, u32[]{:S(2)}, u32[]{:S(2)}) collective-permute-start(bf16[64,512]{1,0:T(8,128)(2,1)S(1)} %slice.41), channel_id=1, source_target_pairs={{0,2},{1,3},{2,0},{3,1},{4,6},{5,7},{6,4},{7,5},{8,10},{9,11},{10,... | collective-permute-start | bytes 196616 | tf_op jit(solution)/shard_map/ppermute | solution.py:32
where the time goes:
time: 106 us
  starting transfers between devices  38.4 us (36%)
  waiting for transfers between devices  34.2 us (32%)
  Pallas kernels  29.1 us (27%)
  local copies, waits for them, and re-layouts  1.97 us (2%)
  between operations  1.61 us (2%)
    ppermute x28, starting transfers between devices, moved(): return lax.ppermute(x, ('cp', 'tp'), pairs)  38.4 us
    ppermute x28, waiting for transfers between devices, moved(): return lax.ppermute(x, ('cp', 'tp'), pairs)  34.2 us
    pallas_call x5, Pallas kernels, attend(): pl.pallas_call(functools.partial(attend_kernel, kvs=kvs, first=first, nb=...  21.2 us
    pallas_call x3, Pallas kernels, project(): pl.pallas_call(project_kernel, in_specs=[vmem] * 3, out_specs=vmem, out_s...  2.53 us
  transfers between devices with their start and end apart: 28, of which 15 were waited for; matrix products, arithmetic and copies ran while one was open for 2% of the time, Pallas kernels for 26%

commit v1 on v0

--- a/solution.py
+++ b/solution.py
@@ -104,9 +104,10 @@
     )(info, k, v)
 
 
-def attend_kernel(q_ref, kx, vx, o_ref, *, kvs, first, nb, tile, scale):
+def attend_kernel(q_ref, kx, vx, *o_refs, kvs, first, nb, tile, scale):
     step = pl.program_id(0)
     span = vx.shape[1]
+    share = nb // len(o_refs)
     eye = diagonal()
 
     def rows_of(b, count):
@@ -125,7 +126,7 @@
     def point(m):
         return jnp.maximum(m * scale, 0.01 * NEG).astype(jnp.bfloat16).astype(jnp.float32)
 
-    def put(b, r, results):
+    def put(o_ref, b, r, results):
         stats = []
         for i, (m, acc) in enumerate(results):
             o_ref[b, i * 128 : (i + 1) * 128, :] = acc[r, :128].astype(jnp.bfloat16)
@@ -144,13 +145,13 @@
         ok.append(jnp.min(jnp.where(acc[:, 128:] < BIG, 1.0, 0.0)))
         results.append((m, acc))
     for b in range(nb):
-        put(b, slice(b * 128, (b + 1) * 128), results)
+        put(o_refs[b // share], b % share, slice(b * 128, (b + 1) * 128), results)
 
     @pl.when(functools.reduce(jnp.minimum, ok) < 0.5)
     def _():
-        def block(b, _):
+        def block(o_ref, at, b, _):
             results = []
-            for q, kv in zip(rows_of(b, 1), kvs):
+            for q, kv in zip(rows_of(at + b, 1), kvs):
 
                 def top(n, m):
                     s = scores(q, kv, pl.multiple_of(n * tile, tile))
@@ -164,13 +165,14 @@
                     return acc + jnp.dot(p, vx[kv, pl.ds(t, tile), :], preferred_element_type=jnp.float32)
 
                 results.append((m, lax.fori_loop(0, span // tile, add, jnp.zeros((128, 256), jnp.float32))))
-            put(b, slice(0, 128), results)
+            put(o_ref, b, slice(0, 128), results)
             return 0
 
-        lax.fori_loop(0, nb, block, 0)
-
-
-def attend(q, kx, vx, kvs, first=0, blocks=8, nb=None):
+        for i, o_ref in enumerate(o_refs):
+            lax.fori_loop(0, share, functools.partial(block, o_ref, i * share), 0)
+
+
+def attend(q, kx, vx, kvs, first=0, blocks=8, nb=None, outs=1):
     span = vx.shape[1]
     nb, tile = nb or blocks, 256
     skip = first // nb
@@ -181,8 +183,8 @@
         ),
         grid=(blocks // nb,),
         in_specs=[pl.BlockSpec((nb, *q.shape[1:]), lambda i: (skip + i, 0, 0, 0)), vmem, vmem],
-        out_specs=pl.BlockSpec((nb, len(kvs) * 136, 128), lambda i: (i, 0, 0)),
-        out_shape=jax.ShapeDtypeStruct((blocks, len(kvs) * 136, 128), jnp.bfloat16),
+        out_specs=[pl.BlockSpec((nb // outs, len(kvs) * 136, 128), lambda i: (i, 0, 0))] * outs,
+        out_shape=[jax.ShapeDtypeStruct((blocks // outs, len(kvs) * 136, 128), jnp.bfloat16)] * outs,
         compiler_params=pltpu.CompilerParams(vmem_limit_bytes=20 * MIB, dimension_semantics=("arbitrary",)),
         cost_estimate=pl.CostEstimate(
             flops=8 * blocks * len(kvs) * 128 * span * 128,
@@ -342,21 +344,19 @@
 
     q2, q1, q3 = (moved(q, b=d) for d in (2, 1, 3))
     kvs = tuple(range(nkv))
-    own = attend(q, kx0, vx, kvs, nb=4)
+    own = attend(q, kx0, vx, kvs, nb=4)[0]
     q2, own = together(q2, own)
-    p2 = attend(q2, kx2, vx, kvs)
+    p2 = attend(q2, kx2, vx, kvs)[0]
     r2 = moved(p2, b=-2)
     q1, q3, p2 = together(q1, q3, p2)
-    p1 = attend(q1, kx1, vx, kvs)
+    p1 = attend(q1, kx1, vx, kvs)[0]
     r1 = moved(p1, b=-1)
     q3, p1 = together(q3, p1)
-    p3a = attend(q3, kx3, vx, kvs, 0, 4)
-    r3a = moved(p3a, b=-3)
-    q3, p3a, r2 = together(q3, p3a, r2)
-    p3b = attend(q3, kx3, vx, kvs, 4, 4)
-    r3b = moved(p3b, b=-3)
+    p3a, p3b = attend(q3, kx3, vx, kvs, outs=2)
+    r3a, r3b = moved(p3a, b=-3), moved(p3b, b=-3)
     low = combine(4, (own, 0), (r1, 0), (r2, 0), (r3a, 0))
     s2 = moved(low[2:], a=-2)
+    own, low = together(own, low)
     high = combine(4, (own, 4), (r1, 4), (r2, 4), (r3b, 0))
     s1, s3 = moved(high[:2], a=-1), moved(high[2:], a=-3)
     c = combine(2, (low, 0), (s1, 0), (s2, 0), (s3, 0))

time: 106 us -> 109 us (1.028)
  waiting for transfers between devices: 34.2 us -> 38.1 us
    ppermute x28, waiting for transfers between devices: 34.2 us -> 38.1 us  [moved(): return lax.ppermute(x, ('cp', 'tp'), pairs)]
    pallas_call x5 -> x4, Pallas kernels: 21.2 us -> 20.3 us  [attend(): pl.pallas_call(functools.partial(attend_kernel, kvs=kvs, first=first, nb=...]
  transfers between devices with their start and end apart: 28 -> 28, of which waited for: 15 -> 17; matrix products, arithmetic and copies ran while one was open for 2% -> 2% of each run, Pallas kernels for 26% -> 23%
where the time goes in v1:
time: 109 us
  starting transfers between devices  38.1 us (35%)
  waiting for transfers between devices  38.1 us (35%)
  Pallas kernels  28.3 us (26%)
  local copies, waits for them, and re-layouts  1.97 us (2%)
  between operations  1.59 us (1%)
    ppermute x28, starting transfers between devices, moved(): return lax.ppermute(x, ('cp', 'tp'), pairs)  38.1 us
    ppermute x28, waiting for transfers between devices, moved(): return lax.ppermute(x, ('cp', 'tp'), pairs)  38.1 us
    pallas_call x4, Pallas kernels, attend(): pl.pallas_call(functools.partial(attend_kernel, kvs=kvs, first=first, nb=...  20.3 us
    pallas_call x3, Pallas kernels, project(): pl.pallas_call(project_kernel, in_specs=[vmem] * 3, out_specs=vmem, out_s...  2.53 us
  transfers between devices with their start and end apart: 28, of which 17 were waited for; matrix products, arithmetic and copies ran while one was open for 2% of the time, Pallas kernels for 23%

profile of v1, /device:TPU:0, one launch (start us, length us, event | category | flops | bytes accessed | tf_op | source)
XLA Modules:
  0.0 108.8 jit_solution(1340031063220069482)
XLA Ops:
  0.0 3.3 %collective-permute-start = (bf16[1,8,32,128]{3,2,1,0:T(8,128)(2,1)}, bf16[1,8,32,128]{3,2,1,0:T(8,128)(2,1)S(1)}, u32[]{:S(2)}, u32[]{:S(2)}) collective-permute-start(bf16[1,8,32,128]{3,2,1,0:T(8,128)(2,1)} %bitcast.10), channel_id=1, source_target_pairs={{0,16},{1,17},{2,18},{3,19},{4,20},{5,21},{6,22},{7,23},{8,24},{9,... | collective-permute-start | bytes 196616 | tf_op jit(solution)/shard_map/ppermute | solution.py:32
  3.3 1.8 %copy_bitcast_fusion = (bf16[2,2048,128]{2,1,0:T(8,128)(2,1)S(1)}, bf16[2,2048,128]{2,1,0:T(8,128)(2,1)S(1)}) fusion(bf16[2048,2,128]{2,1,0:T(2,128)(2,1)} %param.8, bf16[2048,2,128]{2,1,0:T(2,128)(2,1)} %param.7), kind=kLoop, calls=%fused_computation | loop fusion | bytes 4194304 | tf_op jit(solution)/shard_map/transpose | solution.py:336
  6.6 4.0 %collective-permute-start.1 = (bf16[2,8,32,128]{3,2,1,0:T(8,128)(2,1)S(1)}, bf16[2,8,32,128]{3,2,1,0:T(8,128)(2,1)S(1)}, u32[]{:S(2)}, u32[]{:S(2)}) collective-permute-start(bf16[2,8,32,128]{3,2,1,0:T(8,128)(2,1)S(1)} %pad_maximum_fusion.refs_0_), channel_id=1, source_target_pairs={{0,64},{1,9},{2,66},{3,11},{4,68},{5,13},{6,70},{7,15},{8,72},{9,1... | collective-permute-start | bytes 393224 | tf_op jit(solution)/shard_map/ppermute | solution.py:32
  11.5 2.2 %collective-permute-start.3 = (bf16[2,8,32,128]{3,2,1,0:T(8,128)(2,1)S(1)}, bf16[2,8,32,128]{3,2,1,0:T(8,128)(2,1)S(1)}, u32[]{:S(2)}, u32[]{:S(2)}) collective-permute-start(bf16[2,8,32,128]{3,2,1,0:T(8,128)(2,1)S(1)} %pad_maximum_fusion.refs_0_), channel_id=1, source_target_pairs={{0,96},{1,13},{2,98},{3,15},{4,100},{5,1},{6,102},{7,3},{8,104},{9... | collective-permute-start | bytes 393224 | tf_op jit(solution)/shard_map/ppermute | solution.py:32
  13.8 2.0 %prepare.1 = (bf16[2,2048,256]{2,1,0:T(8,128)(2,1)S(1)}, bf16[2,2048,256]{2,1,0:T(8,128)(2,1)S(1)}, bf16[2,2048,256]{2,1,0:T(8,128)(2,1)S(1)}, bf16[2,2048,256]{...) custom-call(s32[7]{0:T(128)S(1)} %concatenate.7.info, bf16[2,2048,128]{2,1,0:T(8,128)(2,1)S(1)} %get-tuple-element.31.k_ref, ...), custom_call_target="tpu_custom_call" | custom-call | tf_op jit(solution)/shard_map/prepare/pallas_call | solution.py:97
  17.2 3.1 %collective-permute-start.5 = (bf16[8,8,32,128]{3,2,1,0:T(8,128)(2,1)S(1)}, bf16[8,8,32,128]{3,2,1,0:T(8,128)(2,1)S(1)}, u32[]{:S(2)}, u32[]{:S(2)}) collective-permute-start(bf16[8,8,32,128]{3,2,1,0:T(8,128)(2,1)S(1)} %assemble.3.q_ref), channel_id=1, source_target_pairs={{0,8},{1,65},{2,10},{3,67},{4,12},{5,69},{6,14},{7,71},{8,0},{9,73... | collective-permute-start | bytes 1572872 | tf_op jit(solution)/shard_map/ppermute | solution.py:32
  20.9 2.6 %collective-permute-start.7 = (bf16[8,8,32,128]{3,2,1,0:T(8,128)(2,1)S(1)}, bf16[8,8,32,128]{3,2,1,0:T(8,128)(2,1)S(1)}, u32[]{:S(2)}, u32[]{:S(2)}) collective-permute-start(bf16[8,8,32,128]{3,2,1,0:T(8,128)(2,1)S(1)} %assemble.3.q_ref), channel_id=1, source_target_pairs={{0,12},{1,97},{2,14},{3,99},{4,0},{5,101},{6,2},{7,103},{8,4},{9,1... | collective-permute-start | bytes 1572872 | tf_op jit(solution)/shard_map/ppermute | solution.py:32
  23.6 5.5 %attend_plane.4.refs_0_ = bf16[8,272,128]{2,1,0:T(8,128)(2,1)S(1)} custom-call(bf16[8,8,32,128]{3,2,1,0:T(8,128)(2,1)S(1)} %assemble.3.q_ref, bf16[2,2048,256]{2,1,0:T(8,128)(2,1)S(1)} %get-tuple-element.39.kx, bf16[2,2048,256]{2,1,0:T(8,128)(2,1)S(1)} %get-tuple-element.40.vx), custom_call_target="tpu_custom_call" | custom-call | flops 4294967296 | bytes 4194304 | tf_op jit(solution)/shard_map/attend_plane/pallas_call | solution.py:180
  29.1 4.9 %attend_plane.5 = bf16[8,272,128]{2,1,0:T(8,128)(2,1)S(1)} custom-call(bf16[8,8,32,128]{3,2,1,0:T(8,128)(2,1)S(1)} %collective-permute-done.5.q_ref, bf16[2,2048,256]{2,1,0:T(8,128)(2,1)S(1)} %get-tuple-element.43.kx, bf16[2,2048,256]{2,1,0:T(8,128)(2,1)S(1)} %get-tuple-element.40.vx), custom_call_target="tpu_custom_call" | custom-call | flops 4294967296 | bytes 4194304 | tf_op jit(solution)/shard_map/attend_plane/pallas_call | solution.py:180
  34.1 2.3 %collective-permute-start.9 = (bf16[8,272,128]{2,1,0:T(8,128)(2,1)S(1)}, bf16[8,272,128]{2,1,0:T(8,128)(2,1)S(1)}, u32[]{:S(2)}, u32[]{:S(2)}) collective-permute-start(bf16[8,272,128]{2,1,0:T(8,128)(2,1)S(1)} %attend_plane.5), channel_id=1, source_target_pairs={{0,8},{1,65},{2,10},{3,67},{4,12},{5,69},{6,14},{7,71},{8,0},{9,73... | collective-permute-start | bytes 1671176 | tf_op jit(solution)/shard_map/ppermute | solution.py:32
  36.3 4.9 %attend_plane.6 = bf16[8,272,128]{2,1,0:T(8,128)(2,1)S(1)} custom-call(bf16[8,8,32,128]{3,2,1,0:T(8,128)(2,1)S(1)} %collective-permute-done.6.q_ref, bf16[2,2048,256]{2,1,0:T(8,128)(2,1)S(1)} %get-tuple-element.45.kx, bf16[2,2048,256]{2,1,0:T(8,128)(2,1)S(1)} %get-tuple-element.40.vx), custom_call_target="tpu_custom_call" | custom-call | flops 4294967296 | bytes 4194304 | tf_op jit(solution)/shard_map/attend_plane/pallas_call | solution.py:180
  41.3 1.2 %collective-permute-start.8 = (bf16[8,272,128]{2,1,0:T(8,128)(2,1)S(1)}, bf16[8,272,128]{2,1,0:T(8,128)(2,1)S(1)}, u32[]{:S(2)}, u32[]{:S(2)}) collective-permute-start(bf16[8,272,128]{2,1,0:T(8,128)(2,1)S(1)} %attend_plane.6), channel_id=1, source_target_pairs={{0,12},{1,97},{2,14},{3,99},{4,0},{5,101},{6,2},{7,103},{8,4},{9,1... | collective-permute-start | bytes 1671176 | tf_op jit(solution)/shard_map/ppermute | solution.py:32
  42.5 4.9 %attend_plane.7 = (bf16[4,272,128]{2,1,0:T(8,128)(2,1)S(1)}, bf16[4,272,128]{2,1,0:T(8,128)(2,1)S(1)}) custom-call(bf16[8,8,32,128]{3,2,1,0:T(8,128)(2,1)S(1)} %collective-permute-done.7.q_ref, bf16[2,2048,256]{2,1,0:T(8,128)(2,1)S(1)} %get-tuple-element.48.kx, bf16[2,2048,256]{2,1,0:T(8,128)(2,1)S(1)} %get-tuple-element.40.vx), custom_call_target="tpu_custom_call" | custom-call | flops 4294967296 | bytes 4194304 | tf_op jit(solution)/shard_map/attend_plane/pallas_call | solution.py:180
  47.4 1.2 %collective-permute-start.10 = (bf16[4,272,128]{2,1,0:T(8,128)(2,1)S(1)}, bf16[4,272,128]{2,1,0:T(8,128)(2,1)S(1)}, u32[]{:S(2)}, u32[]{:S(2)}) collective-permute-start(bf16[4,272,128]{2,1,0:T(8,128)(2,1)S(1)} %get-tuple-element.49), channel_id=1, source_target_pairs={{0,4},{1,33},{2,6},{3,35},{4,8},{5,37},{6,10},{7,39},{8,12},{9,41}... | collective-permute-start | bytes 835592 | tf_op jit(solution)/shard_map/ppermute | solution.py:32
  49.2 6.3 %collective-permute-done.10.refs_3_ = bf16[4,272,128]{2,1,0:T(8,128)(2,1)S(1)} collective-permute-done((bf16[4,272,128]{2,1,0:T(8,128)(2,1)S(1)}, bf16[4,272,128]{2,1,0:T(8,128)(2,1)S(1)}, u32[]{:S(2)}, u32[]{:S(2)}) %collective-permute-start.10) | collective-permute-done | bytes 278560 | tf_op jit(solution)/shard_map/ppermute | solution.py:32
  56.2 2.3 %collective-permute-done.11.refs_3_ = bf16[4,272,128]{2,1,0:T(8,128)(2,1)S(1)} collective-permute-done((bf16[4,272,128]{2,1,0:T(8,128)(2,1)S(1)}, bf16[4,272,128]{2,1,0:T(8,128)(2,1)S(1)}, u32[]{:S(2)}, u32[]{:S(2)}) %collective-permute-start.11) | collective-permute-done | bytes 278560 | tf_op jit(solution)/shard_map/ppermute | solution.py:32
  59.1 2.8 %collective-permute-start.12 = (bf16[2,272,128]{2,1,0:T(8,128)(2,1)S(1)}, bf16[2,272,128]{2,1,0:T(8,128)(2,1)S(1)}, u32[]{:S(2)}, u32[]{:S(2)}) collective-permute-start(bf16[2,272,128]{2,1,0:T(8,128)(2,1)S(1)} %get-tuple-element.54), channel_id=1, source_target_pairs={{0,96},{1,13},{2,98},{3,15},{4,100},{5,1},{6,102},{7,3},{8,104},{9... | collective-permute-start | bytes 417800 | tf_op jit(solution)/shard_map/ppermute | solution.py:32
  62.0 1.5 %collective-permute-start.13 = (bf16[2,272,128]{2,1,0:T(8,128)(2,1)S(1)}, bf16[2,272,128]{2,1,0:T(8,128)(2,1)S(1)}, u32[]{:S(2)}, u32[]{:S(2)}) collective-permute-start(bf16[2,272,128]{2,1,0:T(8,128)(2,1)S(1)} %slice.30), channel_id=1, source_target_pairs={{0,64},{1,9},{2,66},{3,11},{4,68},{5,13},{6,70},{7,15},{8,72},{9,1... | collective-permute-start | bytes 417800 | tf_op jit(solution)/shard_map/ppermute | solution.py:32
  64.6 5.2 %collective-permute-done.14.refs_3_ = bf16[2,272,128]{2,1,0:T(8,128)(2,1)S(1)} collective-permute-done((bf16[2,272,128]{2,1,0:T(8,128)(2,1)S(1)}, bf16[2,272,128]{2,1,0:T(8,128)(2,1)S(1)}, u32[]{:S(2)}, u32[]{:S(2)}) %collective-permute-start.14) | collective-permute-done | bytes 139296 | tf_op jit(solution)/shard_map/ppermute | solution.py:32
  70.1 2.8 %collective-permute-start.15 = (bf16[2,272,128]{2,1,0:T(8,128)(2,1)S(1)}, bf16[2,272,128]{2,1,0:T(8,128)(2,1)S(1)}, u32[]{:S(2)}, u32[]{:S(2)}) collective-permute-start(bf16[2,272,128]{2,1,0:T(8,128)(2,1)S(1)} %combine.5.mine), channel_id=1, source_target_pairs={{0,16},{1,17},{2,18},{3,19},{4,20},{5,21},{6,22},{7,23},{8,24},{9,... | collective-permute-start | bytes 417800 | tf_op jit(solution)/shard_map/ppermute | solution.py:32
  72.9 3.8 %collective-permute-done.15.theirs = bf16[2,272,128]{2,1,0:T(8,128)(2,1)S(1)} collective-permute-done((bf16[2,272,128]{2,1,0:T(8,128)(2,1)S(1)}, bf16[2,272,128]{2,1,0:T(8,128)(2,1)S(1)}, u32[]{:S(2)}, u32[]{:S(2)}) %collective-permute-start.15) | collective-permute-done | bytes 139296 | tf_op jit(solution)/shard_map/ppermute | solution.py:32
  77.5 1.8 %collective-permute-start.19 = (bf16[16,4096]{1,0:T(8,128)(2,1)S(1)}, bf16[16,4096]{1,0:T(8,128)(2,1)S(1)}, u32[]{:S(2)}, u32[]{:S(2)}) collective-permute-start(bf16[16,4096]{1,0:T(8,128)(2,1)S(1)} %finish.1.refs_0_), channel_id=1, source_target_pairs={{0,96},{1,13},{2,98},{3,15},{4,100},{5,1},{6,102},{7,3},{8,104},{9... | collective-permute-start | bytes 393224 | tf_op jit(solution)/shard_map/ppermute | solution.py:32
  80.1 3.6 %collective-permute-done.17.refs_0_ = bf16[16,4096]{1,0:T(8,128)(2,1)S(1)} collective-permute-done((bf16[16,4096]{1,0:T(8,128)(2,1)S(1)}, bf16[16,4096]{1,0:T(8,128)(2,1)S(1)}, u32[]{:S(2)}, u32[]{:S(2)}) %collective-permute-start.17) | collective-permute-done | bytes 131104 | tf_op jit(solution)/shard_map/ppermute | solution.py:32
  86.7 2.1 %collective-permute-start.22 = (bf16[32,4096]{1,0:T(8,128)(2,1)S(1)}, bf16[32,4096]{1,0:T(8,128)(2,1)S(1)}, u32[]{:S(2)}, u32[]{:S(2)}) collective-permute-start(bf16[32,4096]{1,0:T(8,128)(2,1)S(1)} %assemble.4.xa), channel_id=1, source_target_pairs={{0,12},{1,97},{2,14},{3,99},{4,0},{5,101},{6,2},{7,103},{8,4},{9,1... | collective-permute-start | bytes 786440 | tf_op jit(solution)/shard_map/ppermute | solution.py:32
  88.8 2.1 %collective-permute-done.23.xb = bf16[32,4096]{1,0:T(8,128)(2,1)S(1)} collective-permute-done((bf16[32,4096]{1,0:T(8,128)(2,1)S(1)}, bf16[32,4096]{1,0:T(8,128)(2,1)S(1)}, u32[]{:S(2)}, u32[]{:S(2)}) %collective-permute-start.23) | collective-permute-done | bytes 262176 | tf_op jit(solution)/shard_map/ppermute | solution.py:32
  90.9 1.2 %collective-permute-start.25 = (bf16[32,4096]{1,0:T(8,128)(2,1)S(1)}, bf16[32,4096]{1,0:T(8,128)(2,1)S(1)}, u32[]{:S(2)}, u32[]{:S(2)}) collective-permute-start(bf16[32,4096]{1,0:T(8,128)(2,1)S(1)} %collective-permute-done.23.xb), channel_id=1, source_target_pairs={{0,12},{1,97},{2,14},{3,99},{4,0},{5,101},{6,2},{7,103},{8,4},{9,1... | collective-permute-start | bytes 786440 | tf_op jit(solution)/shard_map/ppermute | solution.py:32
  94.9 1.5 %collective-permute-done.21.xb = bf16[32,4096]{1,0:T(8,128)(2,1)S(1)} collective-permute-done((bf16[32,4096]{1,0:T(8,128)(2,1)S(1)}, bf16[32,4096]{1,0:T(8,128)(2,1)S(1)}, u32[]{:S(2)}, u32[]{:S(2)}) %collective-permute-start.21) | collective-permute-done | bytes 262176 | tf_op jit(solution)/shard_map/ppermute | solution.py:32
  97.3 3.4 %collective-permute-done.24.xa = bf16[32,4096]{1,0:T(8,128)(2,1)S(1)} collective-permute-done((bf16[32,4096]{1,0:T(8,128)(2,1)S(1)}, bf16[32,4096]{1,0:T(8,128)(2,1)S(1)}, u32[]{:S(2)}, u32[]{:S(2)}) %collective-permute-start.24) | collective-permute-done | bytes 262176 | tf_op jit(solution)/shard_map/ppermute | solution.py:32
  100.7 1.4 %place.1 = f32[256,512]{1,0:T(8,128)S(1)} custom-call(s32[7]{0:T(128)S(1)} %concatenate.7.info, f32[64,512]{1,0:T(8,128)S(1)} %project.3.y0, f32[64,512]{1,0:T(8,128)S(1)} %project.4.y1, f32[64,512]{1,0:T(8,128)S(1)} %project.5.y3, bf16[32,4096]{1,0:T(8,128)(2,1)S(1)} %collective-permute-done.24.xa, bf16[32,4096]{1,0:T(8,128)(2,1)S(1)} %collective-permute-done.25.xb, ...), custom_call_target="tpu_custom_call" | custom-call | tf_op jit(solution)/shard_map/place/pallas_call | solution.py:321
  102.2 1.5 %collective-permute-done.26 = f32[128,512]{1,0:T(8,128)S(1)} collective-permute-done((f32[128,512]{1,0:T(8,128)S(1)}, f32[128,512]{1,0:T(8,128)S(1)}, u32[]{:S(2)}, u32[]{:S(2)}) %collective-permute-start.26) | collective-permute-done | bytes 262176 | tf_op jit(solution)/shard_map/ppermute | solution.py:32
  103.8 1.2 %collective-permute-start.27 = (bf16[64,512]{1,0:T(8,128)(2,1)S(1)}, bf16[64,512]{1,0:T(8,128)(2,1)S(1)}, u32[]{:S(2)}, u32[]{:S(2)}) collective-permute-start(bf16[64,512]{1,0:T(8,128)(2,1)S(1)} %slice.41), channel_id=1, source_target_pairs={{0,2},{1,3},{2,0},{3,1},{4,6},{5,7},{6,4},{7,5},{8,10},{9,11},{10,... | collective-permute-start | bytes 196616 | tf_op jit(solution)/shard_map/ppermute | solution.py:32
  105.0 3.2 %collective-permute-done.27 = bf16[64,512]{1,0:T(8,128)(2,1)S(1)} collective-permute-done((bf16[64,512]{1,0:T(8,128)(2,1)S(1)}, bf16[64,512]{1,0:T(8,128)(2,1)S(1)}, u32[]{:S(2)}, u32[]{:S(2)}) %collective-permute-start.27) | collective-permute-done | bytes 65568 | tf_op jit(solution)/shard_map/ppermute | solution.py:32
  (53 shorter events, 15.5 us)
Async XLA Ops:
  0.0 6.5 %copy-start.1 = (bf16[8,32,128]{2,1,0:T(8,128)(2,1)S(1)}, bf16[8,32,128]{2,1,0:T(8,128)(2,1)}, u32[]{:S(2)}) copy-start(bf16[8,32,128]{2,1,0:T(8,128)(2,1)} %param.6) | copy-start | bytes 196612
  0.0 6.5 %collective-permute-start = (bf16[1,8,32,128]{3,2,1,0:T(8,128)(2,1)}, bf16[1,8,32,128]{3,2,1,0:T(8,128)(2,1)S(1)}, u32[]{:S(2)}, u32[]{:S(2)}) collective-permute-start(bf16[1,8,32,128]{3,2,1,0:T(8,128)(2,1)} %bitcast.10), channel_id=1, source_target_pairs={{0,16},{1,17},{2,18},{3,19},{4,20},{5,21},{6,22},{7,23},{8,24},{9,... | collective-permute-start | bytes 196616 | tf_op jit(solution)/shard_map/ppermute | solution.py:32
  6.6 9.2 %collective-permute-start.1 = (bf16[2,8,32,128]{3,2,1,0:T(8,128)(2,1)S(1)}, bf16[2,8,32,128]{3,2,1,0:T(8,128)(2,1)S(1)}, u32[]{:S(2)}, u32[]{:S(2)}) collective-permute-start(bf16[2,8,32,128]{3,2,1,0:T(8,128)(2,1)S(1)} %pad_maximum_fusion.refs_0_), channel_id=1, source_target_pairs={{0,64},{1,9},{2,66},{3,11},{4,68},{5,13},{6,70},{7,15},{8,72},{9,1... | collective-permute-start | bytes 393224 | tf_op jit(solution)/shard_map/ppermute | solution.py:32
  10.5 6.2 %collective-permute-start.2 = (bf16[2,8,32,128]{3,2,1,0:T(8,128)(2,1)S(1)}, bf16[2,8,32,128]{3,2,1,0:T(8,128)(2,1)S(1)}, u32[]{:S(2)}, u32[]{:S(2)}) collective-permute-start(bf16[2,8,32,128]{3,2,1,0:T(8,128)(2,1)S(1)} %pad_maximum_fusion.refs_0_), channel_id=1, source_target_pairs={{0,32},{1,5},{2,34},{3,7},{4,36},{5,9},{6,38},{7,11},{8,40},{9,13}... | collective-permute-start | bytes 393224 | tf_op jit(solution)/shard_map/ppermute | solution.py:32
  11.5 5.2 %collective-permute-start.3 = (bf16[2,8,32,128]{3,2,1,0:T(8,128)(2,1)S(1)}, bf16[2,8,32,128]{3,2,1,0:T(8,128)(2,1)S(1)}, u32[]{:S(2)}, u32[]{:S(2)}) collective-permute-start(bf16[2,8,32,128]{3,2,1,0:T(8,128)(2,1)S(1)} %pad_maximum_fusion.refs_0_), channel_id=1, source_target_pairs={{0,96},{1,13},{2,98},{3,15},{4,100},{5,1},{6,102},{7,3},{8,104},{9... | collective-permute-start | bytes 393224 | tf_op jit(solution)/shard_map/ppermute | solution.py:32
  15.7 1.4 %collective-permute-start.4 = (bf16[2,8,32,128]{3,2,1,0:T(8,128)(2,1)S(1)}, bf16[2,8,32,128]{3,2,1,0:T(8,128)(2,1)S(1)}, u32[]{:S(2)}, u32[]{:S(2)}) collective-permute-start(bf16[2,8,32,128]{3,2,1,0:T(8,128)(2,1)S(1)} %collective-permute-done.1.refs_1_), channel_id=1, source_target_pairs={{0,1},{1,0},{2,3},{3,2},{4,5},{5,4},{6,7},{7,6},{8,9},{9,8},{10,11... | collective-permute-start | bytes 393224 | tf_op jit(solution)/shard_map/ppermute | solution.py:32
  17.2 11.9 %collective-permute-start.5 = (bf16[8,8,32,128]{3,2,1,0:T(8,128)(2,1)S(1)}, bf16[8,8,32,128]{3,2,1,0:T(8,128)(2,1)S(1)}, u32[]{:S(2)}, u32[]{:S(2)}) collective-permute-start(bf16[8,8,32,128]{3,2,1,0:T(8,128)(2,1)S(1)} %assemble.3.q_ref), channel_id=1, source_target_pairs={{0,8},{1,65},{2,10},{3,67},{4,12},{5,69},{6,14},{7,71},{8,0},{9,73... | collective-permute-start | bytes 1572872 | tf_op jit(solution)/shard_map/ppermute | solution.py:32
  20.3 16.0 %collective-permute-start.6 = (bf16[8,8,32,128]{3,2,1,0:T(8,128)(2,1)S(1)}, bf16[8,8,32,128]{3,2,1,0:T(8,128)(2,1)S(1)}, u32[]{:S(2)}, u32[]{:S(2)}) collective-permute-start(bf16[8,8,32,128]{3,2,1,0:T(8,128)(2,1)S(1)} %assemble.3.q_ref), channel_id=1, source_target_pairs={{0,4},{1,33},{2,6},{3,35},{4,8},{5,37},{6,10},{7,39},{8,12},{9,41}... | collective-permute-start | bytes 1572872 | tf_op jit(solution)/shard_map/ppermute | solution.py:32
  20.9 15.4 %collective-permute-start.7 = (bf16[8,8,32,128]{3,2,1,0:T(8,128)(2,1)S(1)}, bf16[8,8,32,128]{3,2,1,0:T(8,128)(2,1)S(1)}, u32[]{:S(2)}, u32[]{:S(2)}) collective-permute-start(bf16[8,8,32,128]{3,2,1,0:T(8,128)(2,1)S(1)} %assemble.3.q_ref), channel_id=1, source_target_pairs={{0,12},{1,97},{2,14},{3,99},{4,0},{5,101},{6,2},{7,103},{8,4},{9,1... | collective-permute-start | bytes 1572872 | tf_op jit(solution)/shard_map/ppermute | solution.py:32
  34.1 21.4 %collective-permute-start.9 = (bf16[8,272,128]{2,1,0:T(8,128)(2,1)S(1)}, bf16[8,272,128]{2,1,0:T(8,128)(2,1)S(1)}, u32[]{:S(2)}, u32[]{:S(2)}) collective-permute-start(bf16[8,272,128]{2,1,0:T(8,128)(2,1)S(1)} %attend_plane.5), channel_id=1, source_target_pairs={{0,8},{1,65},{2,10},{3,67},{4,12},{5,69},{6,14},{7,71},{8,0},{9,73... | collective-permute-start | bytes 1671176 | tf_op jit(solution)/shard_map/ppermute | solution.py:32
  41.3 14.2 %collective-permute-start.8 = (bf16[8,272,128]{2,1,0:T(8,128)(2,1)S(1)}, bf16[8,272,128]{2,1,0:T(8,128)(2,1)S(1)}, u32[]{:S(2)}, u32[]{:S(2)}) collective-permute-start(bf16[8,272,128]{2,1,0:T(8,128)(2,1)S(1)} %attend_plane.6), channel_id=1, source_target_pairs={{0,12},{1,97},{2,14},{3,99},{4,0},{5,101},{6,2},{7,103},{8,4},{9,1... | collective-permute-start | bytes 1671176 | tf_op jit(solution)/shard_map/ppermute | solution.py:32
  47.4 8.0 %collective-permute-start.10 = (bf16[4,272,128]{2,1,0:T(8,128)(2,1)S(1)}, bf16[4,272,128]{2,1,0:T(8,128)(2,1)S(1)}, u32[]{:S(2)}, u32[]{:S(2)}) collective-permute-start(bf16[4,272,128]{2,1,0:T(8,128)(2,1)S(1)} %get-tuple-element.49), channel_id=1, source_target_pairs={{0,4},{1,33},{2,6},{3,35},{4,8},{5,37},{6,10},{7,39},{8,12},{9,41}... | collective-permute-start | bytes 835592 | tf_op jit(solution)/shard_map/ppermute | solution.py:32
  48.6 9.9 %collective-permute-start.11 = (bf16[4,272,128]{2,1,0:T(8,128)(2,1)S(1)}, bf16[4,272,128]{2,1,0:T(8,128)(2,1)S(1)}, u32[]{:S(2)}, u32[]{:S(2)}) collective-permute-start(bf16[4,272,128]{2,1,0:T(8,128)(2,1)S(1)} %get-tuple-element.52), channel_id=1, source_target_pairs={{0,4},{1,33},{2,6},{3,35},{4,8},{5,37},{6,10},{7,39},{8,12},{9,41}... | collective-permute-start | bytes 835592 | tf_op jit(solution)/shard_map/ppermute | solution.py:32
  56.2 37.0 %copy-start = (bf16[4096,512]{1,0:T(8,128)(2,1)S(1)}, bf16[4096,512]{1,0:T(8,128)(2,1)}, u32[]{:S(2)}) copy-start(bf16[4096,512]{1,0:T(8,128)(2,1)} %w_ref.7) | copy-start | bytes 12582916
  59.1 5.4 %collective-permute-start.12 = (bf16[2,272,128]{2,1,0:T(8,128)(2,1)S(1)}, bf16[2,272,128]{2,1,0:T(8,128)(2,1)S(1)}, u32[]{:S(2)}, u32[]{:S(2)}) collective-permute-start(bf16[2,272,128]{2,1,0:T(8,128)(2,1)S(1)} %get-tuple-element.54), channel_id=1, source_target_pairs={{0,96},{1,13},{2,98},{3,15},{4,100},{5,1},{6,102},{7,3},{8,104},{9... | collective-permute-start | bytes 417800 | tf_op jit(solution)/shard_map/ppermute | solution.py:32
  62.0 7.8 %collective-permute-start.14 = (bf16[2,272,128]{2,1,0:T(8,128)(2,1)S(1)}, bf16[2,272,128]{2,1,0:T(8,128)(2,1)S(1)}, u32[]{:S(2)}, u32[]{:S(2)}) collective-permute-start(bf16[2,272,128]{2,1,0:T(8,128)(2,1)S(1)} %get-tuple-element.53), channel_id=1, source_target_pairs={{0,32},{1,5},{2,34},{3,7},{4,36},{5,9},{6,38},{7,11},{8,40},{9,13}... | collective-permute-start | bytes 417800 | tf_op jit(solution)/shard_map/ppermute | solution.py:32
  62.0 7.8 %collective-permute-start.13 = (bf16[2,272,128]{2,1,0:T(8,128)(2,1)S(1)}, bf16[2,272,128]{2,1,0:T(8,128)(2,1)S(1)}, u32[]{:S(2)}, u32[]{:S(2)}) collective-permute-start(bf16[2,272,128]{2,1,0:T(8,128)(2,1)S(1)} %slice.30), channel_id=1, source_target_pairs={{0,64},{1,9},{2,66},{3,11},{4,68},{5,13},{6,70},{7,15},{8,72},{9,1... | collective-permute-start | bytes 417800 | tf_op jit(solution)/shard_map/ppermute | solution.py:32
  70.1 6.6 %collective-permute-start.15 = (bf16[2,272,128]{2,1,0:T(8,128)(2,1)S(1)}, bf16[2,272,128]{2,1,0:T(8,128)(2,1)S(1)}, u32[]{:S(2)}, u32[]{:S(2)}) collective-permute-start(bf16[2,272,128]{2,1,0:T(8,128)(2,1)S(1)} %combine.5.mine), channel_id=1, source_target_pairs={{0,16},{1,17},{2,18},{3,19},{4,20},{5,21},{6,22},{7,23},{8,24},{9,... | collective-permute-start | bytes 417800 | tf_op jit(solution)/shard_map/ppermute | solution.py:32
  77.1 6.6 %collective-permute-start.17 = (bf16[16,4096]{1,0:T(8,128)(2,1)S(1)}, bf16[16,4096]{1,0:T(8,128)(2,1)S(1)}, u32[]{:S(2)}, u32[]{:S(2)}) collective-permute-start(bf16[16,4096]{1,0:T(8,128)(2,1)S(1)} %finish.1.refs_0_), channel_id=1, source_target_pairs={{0,64},{1,9},{2,66},{3,11},{4,68},{5,13},{6,70},{7,15},{8,72},{9,1... | collective-permute-start | bytes 393224 | tf_op jit(solution)/shard_map/ppermute | solution.py:32
  77.5 6.9 %collective-permute-start.19 = (bf16[16,4096]{1,0:T(8,128)(2,1)S(1)}, bf16[16,4096]{1,0:T(8,128)(2,1)S(1)}, u32[]{:S(2)}, u32[]{:S(2)}) collective-permute-start(bf16[16,4096]{1,0:T(8,128)(2,1)S(1)} %finish.1.refs_0_), channel_id=1, source_target_pairs={{0,96},{1,13},{2,98},{3,15},{4,100},{5,1},{6,102},{7,3},{8,104},{9... | collective-permute-start | bytes 393224 | tf_op jit(solution)/shard_map/ppermute | solution.py:32
  79.3 6.2 %collective-permute-start.16 = (bf16[16,4096]{1,0:T(8,128)(2,1)S(1)}, bf16[16,4096]{1,0:T(8,128)(2,1)S(1)}, u32[]{:S(2)}, u32[]{:S(2)}) collective-permute-start(bf16[16,4096]{1,0:T(8,128)(2,1)S(1)} %finish.1.refs_0_), channel_id=1, source_target_pairs={{0,32},{1,5},{2,34},{3,7},{4,36},{5,9},{6,38},{7,11},{8,40},{9,13}... | collective-permute-start | bytes 393224 | tf_op jit(solution)/shard_map/ppermute | solution.py:32
  83.6 1.8 %collective-permute-start.18 = (bf16[16,4096]{1,0:T(8,128)(2,1)S(1)}, bf16[16,4096]{1,0:T(8,128)(2,1)S(1)}, u32[]{:S(2)}, u32[]{:S(2)}) collective-permute-start(bf16[16,4096]{1,0:T(8,128)(2,1)S(1)} %collective-permute-done.17.refs_0_), channel_id=1, source_target_pairs={{0,1},{1,0},{2,3},{3,2},{4,5},{5,4},{6,7},{7,6},{8,9},{9,8},{10,11... | collective-permute-start | bytes 393224 | tf_op jit(solution)/shard_map/ppermute | solution.py:32
  84.5 6.4 %collective-permute-start.23 = (bf16[32,4096]{1,0:T(8,128)(2,1)S(1)}, bf16[32,4096]{1,0:T(8,128)(2,1)S(1)}, u32[]{:S(2)}, u32[]{:S(2)}) collective-permute-start(bf16[32,4096]{1,0:T(8,128)(2,1)S(1)} %assemble.5.xb), channel_id=1, source_target_pairs={{0,12},{1,97},{2,14},{3,99},{4,0},{5,101},{6,2},{7,103},{8,4},{9,1... | collective-permute-start | bytes 786440 | tf_op jit(solution)/shard_map/ppermute | solution.py:32
  85.5 7.7 %collective-permute-start.20 = (bf16[32,4096]{1,0:T(8,128)(2,1)S(1)}, bf16[32,4096]{1,0:T(8,128)(2,1)S(1)}, u32[]{:S(2)}, u32[]{:S(2)}) collective-permute-start(bf16[32,4096]{1,0:T(8,128)(2,1)S(1)} %assemble.4.xa), channel_id=1, source_target_pairs={{0,4},{1,33},{2,6},{3,35},{4,8},{5,37},{6,10},{7,39},{8,12},{9,41}... | collective-permute-start | bytes 786440 | tf_op jit(solution)/shard_map/ppermute | solution.py:32
  86.7 7.3 %collective-permute-start.22 = (bf16[32,4096]{1,0:T(8,128)(2,1)S(1)}, bf16[32,4096]{1,0:T(8,128)(2,1)S(1)}, u32[]{:S(2)}, u32[]{:S(2)}) collective-permute-start(bf16[32,4096]{1,0:T(8,128)(2,1)S(1)} %assemble.4.xa), channel_id=1, source_target_pairs={{0,12},{1,97},{2,14},{3,99},{4,0},{5,101},{6,2},{7,103},{8,4},{9,1... | collective-permute-start | bytes 786440 | tf_op jit(solution)/shard_map/ppermute | solution.py:32
  88.8 7.6 %collective-permute-start.21 = (bf16[32,4096]{1,0:T(8,128)(2,1)S(1)}, bf16[32,4096]{1,0:T(8,128)(2,1)S(1)}, u32[]{:S(2)}, u32[]{:S(2)}) collective-permute-start(bf16[32,4096]{1,0:T(8,128)(2,1)S(1)} %assemble.5.xb), channel_id=1, source_target_pairs={{0,4},{1,33},{2,6},{3,35},{4,8},{5,37},{6,10},{7,39},{8,12},{9,41}... | collective-permute-start | bytes 786440 | tf_op jit(solution)/shard_map/ppermute | solution.py:32
  90.9 6.4 %collective-permute-start.25 = (bf16[32,4096]{1,0:T(8,128)(2,1)S(1)}, bf16[32,4096]{1,0:T(8,128)(2,1)S(1)}, u32[]{:S(2)}, u32[]{:S(2)}) collective-permute-start(bf16[32,4096]{1,0:T(8,128)(2,1)S(1)} %collective-permute-done.23.xb), channel_id=1, source_target_pairs={{0,12},{1,97},{2,14},{3,99},{4,0},{5,101},{6,2},{7,103},{8,4},{9,1... | collective-permute-start | bytes 786440 | tf_op jit(solution)/shard_map/ppermute | solution.py:32
  93.1 7.6 %collective-permute-start.24 = (bf16[32,4096]{1,0:T(8,128)(2,1)S(1)}, bf16[32,4096]{1,0:T(8,128)(2,1)S(1)}, u32[]{:S(2)}, u32[]{:S(2)}) collective-permute-start(bf16[32,4096]{1,0:T(8,128)(2,1)S(1)} %collective-permute-done.20.xa), channel_id=1, source_target_pairs={{0,4},{1,33},{2,6},{3,35},{4,8},{5,37},{6,10},{7,39},{8,12},{9,41}... | collective-permute-start | bytes 786440 | tf_op jit(solution)/shard_map/ppermute | solution.py:32
  102.1 1.6 %collective-permute-start.26 = (f32[128,512]{1,0:T(8,128)S(1)}, f32[128,512]{1,0:T(8,128)S(1)}, u32[]{:S(2)}, u32[]{:S(2)}) collective-permute-start(f32[128,512]{1,0:T(8,128)S(1)} %slice.33), channel_id=1, source_target_pairs={{0,1},{1,0},{2,3},{3,2},{4,5},{5,4},{6,7},{7,6},{8,9},{9,8},{10,11... | collective-permute-start | bytes 786440 | tf_op jit(solution)/shard_map/ppermute | solution.py:32
  103.8 4.3 %collective-permute-start.27 = (bf16[64,512]{1,0:T(8,128)(2,1)S(1)}, bf16[64,512]{1,0:T(8,128)(2,1)S(1)}, u32[]{:S(2)}, u32[]{:S(2)}) collective-permute-start(bf16[64,512]{1,0:T(8,128)(2,1)S(1)} %slice.41), channel_id=1, source_target_pairs={{0,2},{1,3},{2,0},{3,1},{4,6},{5,7},{6,4},{7,5},{8,10},{9,11},{10,... | collective-permute-start | bytes 196616 | tf_op jit(solution)/shard_map/ppermute | solution.py:32

commit v2 on v0

--- a/solution.py
+++ b/solution.py
@@ -361,9 +361,9 @@
     s1, s3 = moved(high[:2], a=-1), moved(high[2:], a=-3)
     c = combine(2, (low, 0), (s1, 0), (s2, 0), (s3, 0))
     attn = finish(c, moved(c, yh=1))
-    x2, x1, x3 = (moved(attn, a=d) for d in (2, 1, 3))
-    low = assemble([attn, x1], moved(x2, core=1))
-    high = assemble([x2, x3])
+    x1, x2, x3 = (moved(attn, a=d) for d in (1, 2, 3))
+    low = assemble([attn, x1], moved(x1, core=1))
+    high = assemble([x2, x3], low)
     x1a, x3b = moved(low, b=1), moved(high, b=3)
     x1b, x3a = moved(high, b=1), moved(low, b=3)
     x2a, x2b = moved(x1a, b=1), moved(x3b, b=3)

time: 106 us -> 112 us (1.057)
  waiting for transfers between devices: 34.2 us -> 40.7 us
    ppermute x28, waiting for transfers between devices: 34.2 us -> 40.7 us  [moved(): return lax.ppermute(x, ('cp', 'tp'), pairs)]
  transfers between devices with their start and end apart: 28 -> 28, of which waited for: 15 -> 14; matrix products, arithmetic and copies ran while one was open for 2% -> 2% of each run, Pallas kernels for 26% -> 24%
where the time goes in v2:
time: 112 us
  waiting for transfers between devices  40.7 us (36%)
  starting transfers between devices  37.7 us (34%)
  Pallas kernels  29.2 us (26%)
  local copies, waits for them, and re-layouts  1.97 us (2%)
  between operations  1.6 us (1%)
    ppermute x28, waiting for transfers between devices, moved(): return lax.ppermute(x, ('cp', 'tp'), pairs)  40.7 us
    ppermute x28, starting transfers between devices, moved(): return lax.ppermute(x, ('cp', 'tp'), pairs)  37.7 us
    pallas_call x5, Pallas kernels, attend(): pl.pallas_call(functools.partial(attend_kernel, kvs=kvs, first=first, nb=...  21.2 us
    pallas_call x3, Pallas kernels, project(): pl.pallas_call(project_kernel, in_specs=[vmem] * 3, out_specs=vmem, out_s...  2.54 us
  transfers between devices with their start and end apart: 28, of which 14 were waited for; matrix products, arithmetic and copies ran while one was open for 2% of the time, Pallas kernels for 24%

profile of v2, /device:TPU:0, one launch (start us, length us, event | category | flops | bytes accessed | tf_op | source)
XLA Modules:
  0.0 111.9 jit_solution(13613298912977781114)
XLA Ops:
  0.0 3.3 %collective-permute-start = (bf16[1,8,32,128]{3,2,1,0:T(8,128)(2,1)}, bf16[1,8,32,128]{3,2,1,0:T(8,128)(2,1)S(1)}, u32[]{:S(2)}, u32[]{:S(2)}) collective-permute-start(bf16[1,8,32,128]{3,2,1,0:T(8,128)(2,1)} %bitcast.10), channel_id=1, source_target_pairs={{0,16},{1,17},{2,18},{3,19},{4,20},{5,21},{6,22},{7,23},{8,24},{9,... | collective-permute-start | bytes 196616 | tf_op jit(solution)/shard_map/ppermute | solution.py:32
  3.3 1.8 %copy_bitcast_fusion = (bf16[2,2048,128]{2,1,0:T(8,128)(2,1)S(1)}, bf16[2,2048,128]{2,1,0:T(8,128)(2,1)S(1)}) fusion(bf16[2048,2,128]{2,1,0:T(2,128)(2,1)} %param.8, bf16[2048,2,128]{2,1,0:T(2,128)(2,1)} %param.7), kind=kLoop, calls=%fused_computation | loop fusion | bytes 4194304 | tf_op jit(solution)/shard_map/transpose | solution.py:334
  6.6 4.0 %collective-permute-start.1 = (bf16[2,8,32,128]{3,2,1,0:T(8,128)(2,1)S(1)}, bf16[2,8,32,128]{3,2,1,0:T(8,128)(2,1)S(1)}, u32[]{:S(2)}, u32[]{:S(2)}) collective-permute-start(bf16[2,8,32,128]{3,2,1,0:T(8,128)(2,1)S(1)} %pad_maximum_fusion.refs_0_), channel_id=1, source_target_pairs={{0,64},{1,9},{2,66},{3,11},{4,68},{5,13},{6,70},{7,15},{8,72},{9,1... | collective-permute-start | bytes 393224 | tf_op jit(solution)/shard_map/ppermute | solution.py:32
  11.5 2.2 %collective-permute-start.3 = (bf16[2,8,32,128]{3,2,1,0:T(8,128)(2,1)S(1)}, bf16[2,8,32,128]{3,2,1,0:T(8,128)(2,1)S(1)}, u32[]{:S(2)}, u32[]{:S(2)}) collective-permute-start(bf16[2,8,32,128]{3,2,1,0:T(8,128)(2,1)S(1)} %pad_maximum_fusion.refs_0_), channel_id=1, source_target_pairs={{0,96},{1,13},{2,98},{3,15},{4,100},{5,1},{6,102},{7,3},{8,104},{9... | collective-permute-start | bytes 393224 | tf_op jit(solution)/shard_map/ppermute | solution.py:32
  13.8 2.0 %prepare.1 = (bf16[2,2048,256]{2,1,0:T(8,128)(2,1)S(1)}, bf16[2,2048,256]{2,1,0:T(8,128)(2,1)S(1)}, bf16[2,2048,256]{2,1,0:T(8,128)(2,1)S(1)}, bf16[2,2048,256]{...) custom-call(s32[7]{0:T(128)S(1)} %concatenate.7.info, bf16[2,2048,128]{2,1,0:T(8,128)(2,1)S(1)} %get-tuple-element.29.k_ref, ...), custom_call_target="tpu_custom_call" | custom-call | tf_op jit(solution)/shard_map/prepare/pallas_call | solution.py:97
  17.2 3.1 %collective-permute-start.5 = (bf16[8,8,32,128]{3,2,1,0:T(8,128)(2,1)S(1)}, bf16[8,8,32,128]{3,2,1,0:T(8,128)(2,1)S(1)}, u32[]{:S(2)}, u32[]{:S(2)}) collective-permute-start(bf16[8,8,32,128]{3,2,1,0:T(8,128)(2,1)S(1)} %assemble.3.q_ref), channel_id=1, source_target_pairs={{0,8},{1,65},{2,10},{3,67},{4,12},{5,69},{6,14},{7,71},{8,0},{9,73... | collective-permute-start | bytes 1572872 | tf_op jit(solution)/shard_map/ppermute | solution.py:32
  20.9 2.6 %collective-permute-start.7 = (bf16[8,8,32,128]{3,2,1,0:T(8,128)(2,1)S(1)}, bf16[8,8,32,128]{3,2,1,0:T(8,128)(2,1)S(1)}, u32[]{:S(2)}, u32[]{:S(2)}) collective-permute-start(bf16[8,8,32,128]{3,2,1,0:T(8,128)(2,1)S(1)} %assemble.3.q_ref), channel_id=1, source_target_pairs={{0,12},{1,97},{2,14},{3,99},{4,0},{5,101},{6,2},{7,103},{8,4},{9,1... | collective-permute-start | bytes 1572872 | tf_op jit(solution)/shard_map/ppermute | solution.py:32
  23.6 5.5 %attend_plane.5.refs_0_ = bf16[8,272,128]{2,1,0:T(8,128)(2,1)S(1)} custom-call(bf16[8,8,32,128]{3,2,1,0:T(8,128)(2,1)S(1)} %assemble.3.q_ref, bf16[2,2048,256]{2,1,0:T(8,128)(2,1)S(1)} %get-tuple-element.37.kx, bf16[2,2048,256]{2,1,0:T(8,128)(2,1)S(1)} %get-tuple-element.38.vx), custom_call_target="tpu_custom_call" | custom-call | flops 4294967296 | bytes 4194304 | tf_op jit(solution)/shard_map/attend_plane/pallas_call | solution.py:178
  29.1 4.9 %attend_plane.6 = bf16[8,272,128]{2,1,0:T(8,128)(2,1)S(1)} custom-call(bf16[8,8,32,128]{3,2,1,0:T(8,128)(2,1)S(1)} %collective-permute-done.5.q_ref, bf16[2,2048,256]{2,1,0:T(8,128)(2,1)S(1)} %get-tuple-element.41.kx, bf16[2,2048,256]{2,1,0:T(8,128)(2,1)S(1)} %get-tuple-element.38.vx), custom_call_target="tpu_custom_call" | custom-call | flops 4294967296 | bytes 4194304 | tf_op jit(solution)/shard_map/attend_plane/pallas_call | solution.py:178
  34.1 2.3 %collective-permute-start.9 = (bf16[8,272,128]{2,1,0:T(8,128)(2,1)S(1)}, bf16[8,272,128]{2,1,0:T(8,128)(2,1)S(1)}, u32[]{:S(2)}, u32[]{:S(2)}) collective-permute-start(bf16[8,272,128]{2,1,0:T(8,128)(2,1)S(1)} %attend_plane.6), channel_id=1, source_target_pairs={{0,8},{1,65},{2,10},{3,67},{4,12},{5,69},{6,14},{7,71},{8,0},{9,73... | collective-permute-start | bytes 1671176 | tf_op jit(solution)/shard_map/ppermute | solution.py:32
  36.3 4.9 %attend_plane.7 = bf16[8,272,128]{2,1,0:T(8,128)(2,1)S(1)} custom-call(bf16[8,8,32,128]{3,2,1,0:T(8,128)(2,1)S(1)} %collective-permute-done.6.q_ref, bf16[2,2048,256]{2,1,0:T(8,128)(2,1)S(1)} %get-tuple-element.43.kx, bf16[2,2048,256]{2,1,0:T(8,128)(2,1)S(1)} %get-tuple-element.38.vx), custom_call_target="tpu_custom_call" | custom-call | flops 4294967296 | bytes 4194304 | tf_op jit(solution)/shard_map/attend_plane/pallas_call | solution.py:178
  42.5 2.8 %attend_plane.8 = bf16[4,272,128]{2,1,0:T(8,128)(2,1)S(1)} custom-call(bf16[8,8,32,128]{3,2,1,0:T(8,128)(2,1)S(1)} %collective-permute-done.7.q_ref, bf16[2,2048,256]{2,1,0:T(8,128)(2,1)S(1)} %get-tuple-element.46.kx, bf16[2,2048,256]{2,1,0:T(8,128)(2,1)S(1)} %get-tuple-element.38.vx), custom_call_target="tpu_custom_call" | custom-call | flops 2147483648 | bytes 4194304 | tf_op jit(solution)/shard_map/attend_plane/pallas_call | solution.py:178
  46.2 3.0 %attend_plane.9 = bf16[4,272,128]{2,1,0:T(8,128)(2,1)S(1)} custom-call(bf16[8,8,32,128]{3,2,1,0:T(8,128)(2,1)S(1)} %collective-permute-done.7.q_ref, bf16[2,2048,256]{2,1,0:T(8,128)(2,1)S(1)} %get-tuple-element.46.kx, bf16[2,2048,256]{2,1,0:T(8,128)(2,1)S(1)} %get-tuple-element.38.vx), custom_call_target="tpu_custom_call" | custom-call | flops 2147483648 | bytes 4194304 | tf_op jit(solution)/shard_map/attend_plane/pallas_call | solution.py:178
  49.9 3.2 %collective-permute-done.10.refs_3_ = bf16[4,272,128]{2,1,0:T(8,128)(2,1)S(1)} collective-permute-done((bf16[4,272,128]{2,1,0:T(8,128)(2,1)S(1)}, bf16[4,272,128]{2,1,0:T(8,128)(2,1)S(1)}, u32[]{:S(2)}, u32[]{:S(2)}) %collective-permute-start.10) | collective-permute-done | bytes 278560 | tf_op jit(solution)/shard_map/ppermute | solution.py:32
  53.8 1.4 %collective-permute-start.13 = (bf16[2,272,128]{2,1,0:T(8,128)(2,1)S(1)}, bf16[2,272,128]{2,1,0:T(8,128)(2,1)S(1)}, u32[]{:S(2)}, u32[]{:S(2)}) collective-permute-start(bf16[2,272,128]{2,1,0:T(8,128)(2,1)S(1)} %slice.30), channel_id=1, source_target_pairs={{0,64},{1,9},{2,66},{3,11},{4,68},{5,13},{6,70},{7,15},{8,72},{9,1... | collective-permute-start | bytes 417800 | tf_op jit(solution)/shard_map/ppermute | solution.py:32
  55.1 3.1 %collective-permute-done.11.refs_3_ = bf16[4,272,128]{2,1,0:T(8,128)(2,1)S(1)} collective-permute-done((bf16[4,272,128]{2,1,0:T(8,128)(2,1)S(1)}, bf16[4,272,128]{2,1,0:T(8,128)(2,1)S(1)}, u32[]{:S(2)}, u32[]{:S(2)}) %collective-permute-start.11) | collective-permute-done | bytes 278560 | tf_op jit(solution)/shard_map/ppermute | solution.py:32
  59.0 2.1 %collective-permute-start.12 = (bf16[2,272,128]{2,1,0:T(8,128)(2,1)S(1)}, bf16[2,272,128]{2,1,0:T(8,128)(2,1)S(1)}, u32[]{:S(2)}, u32[]{:S(2)}) collective-permute-start(bf16[2,272,128]{2,1,0:T(8,128)(2,1)S(1)} %get-tuple-element.50), channel_id=1, source_target_pairs={{0,96},{1,13},{2,98},{3,15},{4,100},{5,1},{6,102},{7,3},{8,104},{9... | collective-permute-start | bytes 417800 | tf_op jit(solution)/shard_map/ppermute | solution.py:32
  61.1 3.0 %collective-permute-done.12.refs_1_ = bf16[2,272,128]{2,1,0:T(8,128)(2,1)S(1)} collective-permute-done((bf16[2,272,128]{2,1,0:T(8,128)(2,1)S(1)}, bf16[2,272,128]{2,1,0:T(8,128)(2,1)S(1)}, u32[]{:S(2)}, u32[]{:S(2)}) %collective-permute-start.12) | collective-permute-done | bytes 139296 | tf_op jit(solution)/shard_map/ppermute | solution.py:32
  64.1 3.3 %collective-permute-done.14.refs_3_ = bf16[2,272,128]{2,1,0:T(8,128)(2,1)S(1)} collective-permute-done((bf16[2,272,128]{2,1,0:T(8,128)(2,1)S(1)}, bf16[2,272,128]{2,1,0:T(8,128)(2,1)S(1)}, u32[]{:S(2)}, u32[]{:S(2)}) %collective-permute-start.14) | collective-permute-done | bytes 139296 | tf_op jit(solution)/shard_map/ppermute | solution.py:32
  67.7 2.8 %collective-permute-start.15 = (bf16[2,272,128]{2,1,0:T(8,128)(2,1)S(1)}, bf16[2,272,128]{2,1,0:T(8,128)(2,1)S(1)}, u32[]{:S(2)}, u32[]{:S(2)}) collective-permute-start(bf16[2,272,128]{2,1,0:T(8,128)(2,1)S(1)} %combine.5.mine), channel_id=1, source_target_pairs={{0,16},{1,17},{2,18},{3,19},{4,20},{5,21},{6,22},{7,23},{8,24},{9,... | collective-permute-start | bytes 417800 | tf_op jit(solution)/shard_map/ppermute | solution.py:32
  70.5 3.8 %collective-permute-done.15.theirs = bf16[2,272,128]{2,1,0:T(8,128)(2,1)S(1)} collective-permute-done((bf16[2,272,128]{2,1,0:T(8,128)(2,1)S(1)}, bf16[2,272,128]{2,1,0:T(8,128)(2,1)S(1)}, u32[]{:S(2)}, u32[]{:S(2)}) %collective-permute-start.15) | collective-permute-done | bytes 139296 | tf_op jit(solution)/shard_map/ppermute | solution.py:32
  74.8 6.2 %collective-permute-done.16.refs_1_ = bf16[16,4096]{1,0:T(8,128)(2,1)S(1)} collective-permute-done((bf16[16,4096]{1,0:T(8,128)(2,1)S(1)}, bf16[16,4096]{1,0:T(8,128)(2,1)S(1)}, u32[]{:S(2)}, u32[]{:S(2)}) %collective-permute-start.16) | collective-permute-done | bytes 131104 | tf_op jit(solution)/shard_map/ppermute | solution.py:32
  81.0 1.5 %collective-permute-start.19 = (bf16[16,4096]{1,0:T(8,128)(2,1)S(1)}, bf16[16,4096]{1,0:T(8,128)(2,1)S(1)}, u32[]{:S(2)}, u32[]{:S(2)}) collective-permute-start(bf16[16,4096]{1,0:T(8,128)(2,1)S(1)} %finish.1.refs_0_), channel_id=1, source_target_pairs={{0,96},{1,13},{2,98},{3,15},{4,100},{5,1},{6,102},{7,3},{8,104},{9... | collective-permute-start | bytes 393224 | tf_op jit(solution)/shard_map/ppermute | solution.py:32
  82.4 5.0 %collective-permute-done.18.refs_0_ = bf16[16,4096]{1,0:T(8,128)(2,1)S(1)} collective-permute-done((bf16[16,4096]{1,0:T(8,128)(2,1)S(1)}, bf16[16,4096]{1,0:T(8,128)(2,1)S(1)}, u32[]{:S(2)}, u32[]{:S(2)}) %collective-permute-start.18) | collective-permute-done | bytes 131104 | tf_op jit(solution)/shard_map/ppermute | solution.py:32
  89.5 2.3 %collective-permute-start.22 = (bf16[32,4096]{1,0:T(8,128)(2,1)S(1)}, bf16[32,4096]{1,0:T(8,128)(2,1)S(1)}, u32[]{:S(2)}, u32[]{:S(2)}) collective-permute-start(bf16[32,4096]{1,0:T(8,128)(2,1)S(1)} %assemble.4.refs_2_.xa), channel_id=1, source_target_pairs={{0,12},{1,97},{2,14},{3,99},{4,0},{5,101},{6,2},{7,103},{8,4},{9,1... | collective-permute-start | bytes 786440 | tf_op jit(solution)/shard_map/ppermute | solution.py:32
  91.8 2.1 %collective-permute-done.23.xb = bf16[32,4096]{1,0:T(8,128)(2,1)S(1)} collective-permute-done((bf16[32,4096]{1,0:T(8,128)(2,1)S(1)}, bf16[32,4096]{1,0:T(8,128)(2,1)S(1)}, u32[]{:S(2)}, u32[]{:S(2)}) %collective-permute-start.23) | collective-permute-done | bytes 262176 | tf_op jit(solution)/shard_map/ppermute | solution.py:32
  93.9 2.3 %collective-permute-start.25 = (bf16[32,4096]{1,0:T(8,128)(2,1)S(1)}, bf16[32,4096]{1,0:T(8,128)(2,1)S(1)}, u32[]{:S(2)}, u32[]{:S(2)}) collective-permute-start(bf16[32,4096]{1,0:T(8,128)(2,1)S(1)} %collective-permute-done.23.xb), channel_id=1, source_target_pairs={{0,12},{1,97},{2,14},{3,99},{4,0},{5,101},{6,2},{7,103},{8,4},{9,1... | collective-permute-start | bytes 786440 | tf_op jit(solution)/shard_map/ppermute | solution.py:32
  97.9 1.5 %collective-permute-done.21.xb = bf16[32,4096]{1,0:T(8,128)(2,1)S(1)} collective-permute-done((bf16[32,4096]{1,0:T(8,128)(2,1)S(1)}, bf16[32,4096]{1,0:T(8,128)(2,1)S(1)}, u32[]{:S(2)}, u32[]{:S(2)}) %collective-permute-start.21) | collective-permute-done | bytes 262176 | tf_op jit(solution)/shard_map/ppermute | solution.py:32
  100.3 3.5 %collective-permute-done.24.xa = bf16[32,4096]{1,0:T(8,128)(2,1)S(1)} collective-permute-done((bf16[32,4096]{1,0:T(8,128)(2,1)S(1)}, bf16[32,4096]{1,0:T(8,128)(2,1)S(1)}, u32[]{:S(2)}, u32[]{:S(2)}) %collective-permute-start.24) | collective-permute-done | bytes 262176 | tf_op jit(solution)/shard_map/ppermute | solution.py:32
  103.8 1.4 %place.1 = f32[256,512]{1,0:T(8,128)S(1)} custom-call(s32[7]{0:T(128)S(1)} %concatenate.7.info, f32[64,512]{1,0:T(8,128)S(1)} %project.3.y0, f32[64,512]{1,0:T(8,128)S(1)} %project.4.y1, f32[64,512]{1,0:T(8,128)S(1)} %project.5.y3, bf16[32,4096]{1,0:T(8,128)(2,1)S(1)} %collective-permute-done.24.xa, bf16[32,4096]{1,0:T(8,128)(2,1)S(1)} %collective-permute-done.25.xb, ...), custom_call_target="tpu_custom_call" | custom-call | tf_op jit(solution)/shard_map/place/pallas_call | solution.py:319
  105.3 1.5 %collective-permute-done.26 = f32[128,512]{1,0:T(8,128)S(1)} collective-permute-done((f32[128,512]{1,0:T(8,128)S(1)}, f32[128,512]{1,0:T(8,128)S(1)}, u32[]{:S(2)}, u32[]{:S(2)}) %collective-permute-start.26) | collective-permute-done | bytes 262176 | tf_op jit(solution)/shard_map/ppermute | solution.py:32
  108.1 3.2 %collective-permute-done.27 = bf16[64,512]{1,0:T(8,128)(2,1)S(1)} collective-permute-done((bf16[64,512]{1,0:T(8,128)(2,1)S(1)}, bf16[64,512]{1,0:T(8,128)(2,1)S(1)}, u32[]{:S(2)}, u32[]{:S(2)}) %collective-permute-start.27) | collective-permute-done | bytes 65568 | tf_op jit(solution)/shard_map/ppermute | solution.py:32
  (54 shorter events, 14.8 us)
Async XLA Ops:
  0.0 6.5 %copy-start.1 = (bf16[8,32,128]{2,1,0:T(8,128)(2,1)S(1)}, bf16[8,32,128]{2,1,0:T(8,128)(2,1)}, u32[]{:S(2)}) copy-start(bf16[8,32,128]{2,1,0:T(8,128)(2,1)} %param.6) | copy-start | bytes 196612
  0.0 6.5 %collective-permute-start = (bf16[1,8,32,128]{3,2,1,0:T(8,128)(2,1)}, bf16[1,8,32,128]{3,2,1,0:T(8,128)(2,1)S(1)}, u32[]{:S(2)}, u32[]{:S(2)}) collective-permute-start(bf16[1,8,32,128]{3,2,1,0:T(8,128)(2,1)} %bitcast.10), channel_id=1, source_target_pairs={{0,16},{1,17},{2,18},{3,19},{4,20},{5,21},{6,22},{7,23},{8,24},{9,... | collective-permute-start | bytes 196616 | tf_op jit(solution)/shard_map/ppermute | solution.py:32
  6.6 9.2 %collective-permute-start.1 = (bf16[2,8,32,128]{3,2,1,0:T(8,128)(2,1)S(1)}, bf16[2,8,32,128]{3,2,1,0:T(8,128)(2,1)S(1)}, u32[]{:S(2)}, u32[]{:S(2)}) collective-permute-start(bf16[2,8,32,128]{3,2,1,0:T(8,128)(2,1)S(1)} %pad_maximum_fusion.refs_0_), channel_id=1, source_target_pairs={{0,64},{1,9},{2,66},{3,11},{4,68},{5,13},{6,70},{7,15},{8,72},{9,1... | collective-permute-start | bytes 393224 | tf_op jit(solution)/shard_map/ppermute | solution.py:32
  10.5 6.2 %collective-permute-start.2 = (bf16[2,8,32,128]{3,2,1,0:T(8,128)(2,1)S(1)}, bf16[2,8,32,128]{3,2,1,0:T(8,128)(2,1)S(1)}, u32[]{:S(2)}, u32[]{:S(2)}) collective-permute-start(bf16[2,8,32,128]{3,2,1,0:T(8,128)(2,1)S(1)} %pad_maximum_fusion.refs_0_), channel_id=1, source_target_pairs={{0,32},{1,5},{2,34},{3,7},{4,36},{5,9},{6,38},{7,11},{8,40},{9,13}... | collective-permute-start | bytes 393224 | tf_op jit(solution)/shard_map/ppermute | solution.py:32
  11.5 5.2 %collective-permute-start.3 = (bf16[2,8,32,128]{3,2,1,0:T(8,128)(2,1)S(1)}, bf16[2,8,32,128]{3,2,1,0:T(8,128)(2,1)S(1)}, u32[]{:S(2)}, u32[]{:S(2)}) collective-permute-start(bf16[2,8,32,128]{3,2,1,0:T(8,128)(2,1)S(1)} %pad_maximum_fusion.refs_0_), channel_id=1, source_target_pairs={{0,96},{1,13},{2,98},{3,15},{4,100},{5,1},{6,102},{7,3},{8,104},{9... | collective-permute-start | bytes 393224 | tf_op jit(solution)/shard_map/ppermute | solution.py:32
  15.7 1.4 %collective-permute-start.4 = (bf16[2,8,32,128]{3,2,1,0:T(8,128)(2,1)S(1)}, bf16[2,8,32,128]{3,2,1,0:T(8,128)(2,1)S(1)}, u32[]{:S(2)}, u32[]{:S(2)}) collective-permute-start(bf16[2,8,32,128]{3,2,1,0:T(8,128)(2,1)S(1)} %collective-permute-done.1.refs_1_), channel_id=1, source_target_pairs={{0,1},{1,0},{2,3},{3,2},{4,5},{5,4},{6,7},{7,6},{8,9},{9,8},{10,11... | collective-permute-start | bytes 393224 | tf_op jit(solution)/shard_map/ppermute | solution.py:32
  17.2 11.9 %collective-permute-start.5 = (bf16[8,8,32,128]{3,2,1,0:T(8,128)(2,1)S(1)}, bf16[8,8,32,128]{3,2,1,0:T(8,128)(2,1)S(1)}, u32[]{:S(2)}, u32[]{:S(2)}) collective-permute-start(bf16[8,8,32,128]{3,2,1,0:T(8,128)(2,1)S(1)} %assemble.3.q_ref), channel_id=1, source_target_pairs={{0,8},{1,65},{2,10},{3,67},{4,12},{5,69},{6,14},{7,71},{8,0},{9,73... | collective-permute-start | bytes 1572872 | tf_op jit(solution)/shard_map/ppermute | solution.py:32
  20.3 16.0 %collective-permute-start.6 = (bf16[8,8,32,128]{3,2,1,0:T(8,128)(2,1)S(1)}, bf16[8,8,32,128]{3,2,1,0:T(8,128)(2,1)S(1)}, u32[]{:S(2)}, u32[]{:S(2)}) collective-permute-start(bf16[8,8,32,128]{3,2,1,0:T(8,128)(2,1)S(1)} %assemble.3.q_ref), channel_id=1, source_target_pairs={{0,4},{1,33},{2,6},{3,35},{4,8},{5,37},{6,10},{7,39},{8,12},{9,41}... | collective-permute-start | bytes 1572872 | tf_op jit(solution)/shard_map/ppermute | solution.py:32
  20.9 15.4 %collective-permute-start.7 = (bf16[8,8,32,128]{3,2,1,0:T(8,128)(2,1)S(1)}, bf16[8,8,32,128]{3,2,1,0:T(8,128)(2,1)S(1)}, u32[]{:S(2)}, u32[]{:S(2)}) collective-permute-start(bf16[8,8,32,128]{3,2,1,0:T(8,128)(2,1)S(1)} %assemble.3.q_ref), channel_id=1, source_target_pairs={{0,12},{1,97},{2,14},{3,99},{4,0},{5,101},{6,2},{7,103},{8,4},{9,1... | collective-permute-start | bytes 1572872 | tf_op jit(solution)/shard_map/ppermute | solution.py:32
  34.1 12.1 %collective-permute-start.9 = (bf16[8,272,128]{2,1,0:T(8,128)(2,1)S(1)}, bf16[8,272,128]{2,1,0:T(8,128)(2,1)S(1)}, u32[]{:S(2)}, u32[]{:S(2)}) collective-permute-start(bf16[8,272,128]{2,1,0:T(8,128)(2,1)S(1)} %attend_plane.6), channel_id=1, source_target_pairs={{0,8},{1,65},{2,10},{3,67},{4,12},{5,69},{6,14},{7,71},{8,0},{9,73... | collective-permute-start | bytes 1671176 | tf_op jit(solution)/shard_map/ppermute | solution.py:32
  41.3 11.8 %collective-permute-start.8 = (bf16[8,272,128]{2,1,0:T(8,128)(2,1)S(1)}, bf16[8,272,128]{2,1,0:T(8,128)(2,1)S(1)}, u32[]{:S(2)}, u32[]{:S(2)}) collective-permute-start(bf16[8,272,128]{2,1,0:T(8,128)(2,1)S(1)} %attend_plane.7), channel_id=1, source_target_pairs={{0,12},{1,97},{2,14},{3,99},{4,0},{5,101},{6,2},{7,103},{8,4},{9,1... | collective-permute-start | bytes 1671176 | tf_op jit(solution)/shard_map/ppermute | solution.py:32
  45.2 7.8 %collective-permute-start.10 = (bf16[4,272,128]{2,1,0:T(8,128)(2,1)S(1)}, bf16[4,272,128]{2,1,0:T(8,128)(2,1)S(1)}, u32[]{:S(2)}, u32[]{:S(2)}) collective-permute-start(bf16[4,272,128]{2,1,0:T(8,128)(2,1)S(1)} %attend_plane.8), channel_id=1, source_target_pairs={{0,4},{1,33},{2,6},{3,35},{4,8},{5,37},{6,10},{7,39},{8,12},{9,41}... | collective-permute-start | bytes 835592 | tf_op jit(solution)/shard_map/ppermute | solution.py:32
  49.2 9.1 %collective-permute-start.11 = (bf16[4,272,128]{2,1,0:T(8,128)(2,1)S(1)}, bf16[4,272,128]{2,1,0:T(8,128)(2,1)S(1)}, u32[]{:S(2)}, u32[]{:S(2)}) collective-permute-start(bf16[4,272,128]{2,1,0:T(8,128)(2,1)S(1)} %attend_plane.9), channel_id=1, source_target_pairs={{0,4},{1,33},{2,6},{3,35},{4,8},{5,37},{6,10},{7,39},{8,12},{9,41}... | collective-permute-start | bytes 835592 | tf_op jit(solution)/shard_map/ppermute | solution.py:32
  53.8 7.3 %collective-permute-start.13 = (bf16[2,272,128]{2,1,0:T(8,128)(2,1)S(1)}, bf16[2,272,128]{2,1,0:T(8,128)(2,1)S(1)}, u32[]{:S(2)}, u32[]{:S(2)}) collective-permute-start(bf16[2,272,128]{2,1,0:T(8,128)(2,1)S(1)} %slice.30), channel_id=1, source_target_pairs={{0,64},{1,9},{2,66},{3,11},{4,68},{5,13},{6,70},{7,15},{8,72},{9,1... | collective-permute-start | bytes 417800 | tf_op jit(solution)/shard_map/ppermute | solution.py:32
  58.3 37.9 %copy-start = (bf16[4096,512]{1,0:T(8,128)(2,1)S(1)}, bf16[4096,512]{1,0:T(8,128)(2,1)}, u32[]{:S(2)}) copy-start(bf16[4096,512]{1,0:T(8,128)(2,1)} %w_ref.7) | copy-start | bytes 12582916
  59.0 5.1 %collective-permute-start.12 = (bf16[2,272,128]{2,1,0:T(8,128)(2,1)S(1)}, bf16[2,272,128]{2,1,0:T(8,128)(2,1)S(1)}, u32[]{:S(2)}, u32[]{:S(2)}) collective-permute-start(bf16[2,272,128]{2,1,0:T(8,128)(2,1)S(1)} %get-tuple-element.50), channel_id=1, source_target_pairs={{0,96},{1,13},{2,98},{3,15},{4,100},{5,1},{6,102},{7,3},{8,104},{9... | collective-permute-start | bytes 417800 | tf_op jit(solution)/shard_map/ppermute | solution.py:32
  61.1 6.3 %collective-permute-start.14 = (bf16[2,272,128]{2,1,0:T(8,128)(2,1)S(1)}, bf16[2,272,128]{2,1,0:T(8,128)(2,1)S(1)}, u32[]{:S(2)}, u32[]{:S(2)}) collective-permute-start(bf16[2,272,128]{2,1,0:T(8,128)(2,1)S(1)} %get-tuple-element.49), channel_id=1, source_target_pairs={{0,32},{1,5},{2,34},{3,7},{4,36},{5,9},{6,38},{7,11},{8,40},{9,13}... | collective-permute-start | bytes 417800 | tf_op jit(solution)/shard_map/ppermute | solution.py:32
  67.7 6.6 %collective-permute-start.15 = (bf16[2,272,128]{2,1,0:T(8,128)(2,1)S(1)}, bf16[2,272,128]{2,1,0:T(8,128)(2,1)S(1)}, u32[]{:S(2)}, u32[]{:S(2)}) collective-permute-start(bf16[2,272,128]{2,1,0:T(8,128)(2,1)S(1)} %combine.5.mine), channel_id=1, source_target_pairs={{0,16},{1,17},{2,18},{3,19},{4,20},{5,21},{6,22},{7,23},{8,24},{9,... | collective-permute-start | bytes 417800 | tf_op jit(solution)/shard_map/ppermute | solution.py:32
  74.7 6.2 %collective-permute-start.16 = (bf16[16,4096]{1,0:T(8,128)(2,1)S(1)}, bf16[16,4096]{1,0:T(8,128)(2,1)S(1)}, u32[]{:S(2)}, u32[]{:S(2)}) collective-permute-start(bf16[16,4096]{1,0:T(8,128)(2,1)S(1)} %finish.1.refs_0_), channel_id=1, source_target_pairs={{0,32},{1,5},{2,34},{3,7},{4,36},{5,9},{6,38},{7,11},{8,40},{9,13}... | collective-permute-start | bytes 393224 | tf_op jit(solution)/shard_map/ppermute | solution.py:32
  81.0 1.5 %collective-permute-start.17 = (bf16[16,4096]{1,0:T(8,128)(2,1)S(1)}, bf16[16,4096]{1,0:T(8,128)(2,1)S(1)}, u32[]{:S(2)}, u32[]{:S(2)}) collective-permute-start(bf16[16,4096]{1,0:T(8,128)(2,1)S(1)} %collective-permute-done.16.refs_1_), channel_id=1, source_target_pairs={{0,1},{1,0},{2,3},{3,2},{4,5},{5,4},{6,7},{7,6},{8,9},{9,8},{10,11... | collective-permute-start | bytes 393224 | tf_op jit(solution)/shard_map/ppermute | solution.py:32
  81.0 6.5 %collective-permute-start.18 = (bf16[16,4096]{1,0:T(8,128)(2,1)S(1)}, bf16[16,4096]{1,0:T(8,128)(2,1)S(1)}, u32[]{:S(2)}, u32[]{:S(2)}) collective-permute-start(bf16[16,4096]{1,0:T(8,128)(2,1)S(1)} %finish.1.refs_0_), channel_id=1, source_target_pairs={{0,64},{1,9},{2,66},{3,11},{4,68},{5,13},{6,70},{7,15},{8,72},{9,1... | collective-permute-start | bytes 393224 | tf_op jit(solution)/shard_map/ppermute | solution.py:32
  81.0 6.5 %collective-permute-start.19 = (bf16[16,4096]{1,0:T(8,128)(2,1)S(1)}, bf16[16,4096]{1,0:T(8,128)(2,1)S(1)}, u32[]{:S(2)}, u32[]{:S(2)}) collective-permute-start(bf16[16,4096]{1,0:T(8,128)(2,1)S(1)} %finish.1.refs_0_), channel_id=1, source_target_pairs={{0,96},{1,13},{2,98},{3,15},{4,100},{5,1},{6,102},{7,3},{8,104},{9... | collective-permute-start | bytes 393224 | tf_op jit(solution)/shard_map/ppermute | solution.py:32
  87.5 6.4 %collective-permute-start.23 = (bf16[32,4096]{1,0:T(8,128)(2,1)S(1)}, bf16[32,4096]{1,0:T(8,128)(2,1)S(1)}, u32[]{:S(2)}, u32[]{:S(2)}) collective-permute-start(bf16[32,4096]{1,0:T(8,128)(2,1)S(1)} %assemble.5.xb), channel_id=1, source_target_pairs={{0,12},{1,97},{2,14},{3,99},{4,0},{5,101},{6,2},{7,103},{8,4},{9,1... | collective-permute-start | bytes 786440 | tf_op jit(solution)/shard_map/ppermute | solution.py:32
  88.6 7.6 %collective-permute-start.20 = (bf16[32,4096]{1,0:T(8,128)(2,1)S(1)}, bf16[32,4096]{1,0:T(8,128)(2,1)S(1)}, u32[]{:S(2)}, u32[]{:S(2)}) collective-permute-start(bf16[32,4096]{1,0:T(8,128)(2,1)S(1)} %assemble.4.refs_2_.xa), channel_id=1, source_target_pairs={{0,4},{1,33},{2,6},{3,35},{4,8},{5,37},{6,10},{7,39},{8,12},{9,41}... | collective-permute-start | bytes 786440 | tf_op jit(solution)/shard_map/ppermute | solution.py:32
  89.5 7.5 %collective-permute-start.22 = (bf16[32,4096]{1,0:T(8,128)(2,1)S(1)}, bf16[32,4096]{1,0:T(8,128)(2,1)S(1)}, u32[]{:S(2)}, u32[]{:S(2)}) collective-permute-start(bf16[32,4096]{1,0:T(8,128)(2,1)S(1)} %assemble.4.refs_2_.xa), channel_id=1, source_target_pairs={{0,12},{1,97},{2,14},{3,99},{4,0},{5,101},{6,2},{7,103},{8,4},{9,1... | collective-permute-start | bytes 786440 | tf_op jit(solution)/shard_map/ppermute | solution.py:32
  91.8 7.6 %collective-permute-start.21 = (bf16[32,4096]{1,0:T(8,128)(2,1)S(1)}, bf16[32,4096]{1,0:T(8,128)(2,1)S(1)}, u32[]{:S(2)}, u32[]{:S(2)}) collective-permute-start(bf16[32,4096]{1,0:T(8,128)(2,1)S(1)} %assemble.5.xb), channel_id=1, source_target_pairs={{0,4},{1,33},{2,6},{3,35},{4,8},{5,37},{6,10},{7,39},{8,12},{9,41}... | collective-permute-start | bytes 786440 | tf_op jit(solution)/shard_map/ppermute | solution.py:32
  93.9 6.4 %collective-permute-start.25 = (bf16[32,4096]{1,0:T(8,128)(2,1)S(1)}, bf16[32,4096]{1,0:T(8,128)(2,1)S(1)}, u32[]{:S(2)}, u32[]{:S(2)}) collective-permute-start(bf16[32,4096]{1,0:T(8,128)(2,1)S(1)} %collective-permute-done.23.xb), channel_id=1, source_target_pairs={{0,12},{1,97},{2,14},{3,99},{4,0},{5,101},{6,2},{7,103},{8,4},{9,1... | collective-permute-start | bytes 786440 | tf_op jit(solution)/shard_map/ppermute | solution.py:32
  96.2 7.6 %collective-permute-start.24 = (bf16[32,4096]{1,0:T(8,128)(2,1)S(1)}, bf16[32,4096]{1,0:T(8,128)(2,1)S(1)}, u32[]{:S(2)}, u32[]{:S(2)}) collective-permute-start(bf16[32,4096]{1,0:T(8,128)(2,1)S(1)} %collective-permute-done.20.xa), channel_id=1, source_target_pairs={{0,4},{1,33},{2,6},{3,35},{4,8},{5,37},{6,10},{7,39},{8,12},{9,41}... | collective-permute-start | bytes 786440 | tf_op jit(solution)/shard_map/ppermute | solution.py:32
  105.2 1.6 %collective-permute-start.26 = (f32[128,512]{1,0:T(8,128)S(1)}, f32[128,512]{1,0:T(8,128)S(1)}, u32[]{:S(2)}, u32[]{:S(2)}) collective-permute-start(f32[128,512]{1,0:T(8,128)S(1)} %slice.33), channel_id=1, source_target_pairs={{0,1},{1,0},{2,3},{3,2},{4,5},{5,4},{6,7},{7,6},{8,9},{9,8},{10,11... | collective-permute-start | bytes 786440 | tf_op jit(solution)/shard_map/ppermute | solution.py:32
  106.9 4.3 %collective-permute-start.27 = (bf16[64,512]{1,0:T(8,128)(2,1)S(1)}, bf16[64,512]{1,0:T(8,128)(2,1)S(1)}, u32[]{:S(2)}, u32[]{:S(2)}) collective-permute-start(bf16[64,512]{1,0:T(8,128)(2,1)S(1)} %slice.41), channel_id=1, source_target_pairs={{0,2},{1,3},{2,0},{3,1},{4,6},{5,7},{6,4},{7,5},{8,10},{9,11},{10,... | collective-permute-start | bytes 196616 | tf_op jit(solution)/shard_map/ppermute | solution.py:32

commit v3 on v0

--- a/solution.py
+++ b/solution.py
@@ -369,7 +369,7 @@
     x2a, x2b = moved(x1a, b=1), moved(x3b, b=3)
     ys = [project(xa, xb, out_weight) for xa, xb in ((low, high), (x1a, x1b), (x3a, x3b))]
     y = place(info, *ys, x2a, x2b, out_weight)
-    y = y[:128] + moved(y[128:], core=1)
+    y = y[:128] + moved(y[128:].astype(jnp.bfloat16), core=1).astype(jnp.float32)
     y = y[:64] + moved(y[64:].astype(jnp.bfloat16), yl=1).astype(jnp.float32)
     return y.astype(jnp.bfloat16)
 

time: 106 us -> 106 us (level)
  no operation moved by 1% of the time
where the time goes in v3:
time: 106 us
  starting transfers between devices  38.4 us (36%)
  waiting for transfers between devices  34 us (32%)
  Pallas kernels  29.1 us (27%)
  local copies, waits for them, and re-layouts  1.97 us (2%)
  between operations  1.61 us (2%)
    ppermute x28, starting transfers between devices, moved(): return lax.ppermute(x, ('cp', 'tp'), pairs)  38.4 us
    ppermute x28, waiting for transfers between devices, moved(): return lax.ppermute(x, ('cp', 'tp'), pairs)  34 us
    pallas_call x5, Pallas kernels, attend(): pl.pallas_call(functools.partial(attend_kernel, kvs=kvs, first=first, nb=...  21.2 us
    pallas_call x3, Pallas kernels, project(): pl.pallas_call(project_kernel, in_specs=[vmem] * 3, out_specs=vmem, out_s...  2.53 us
  transfers between devices with their start and end apart: 28, of which 15 were waited for; matrix products, arithmetic and copies ran while one was open for 2% of the time, Pallas kernels for 26%

profile of v3, /device:TPU:0, one launch (start us, length us, event | category | flops | bytes accessed | tf_op | source)
XLA Modules:
  0.0 105.8 jit_solution(14892089541337938549)
XLA Ops:
  0.0 3.3 %collective-permute-start = (bf16[1,8,32,128]{3,2,1,0:T(8,128)(2,1)}, bf16[1,8,32,128]{3,2,1,0:T(8,128)(2,1)S(1)}, u32[]{:S(2)}, u32[]{:S(2)}) collective-permute-start(bf16[1,8,32,128]{3,2,1,0:T(8,128)(2,1)} %bitcast.10), channel_id=1, source_target_pairs={{0,16},{1,17},{2,18},{3,19},{4,20},{5,21},{6,22},{7,23},{8,24},{9,... | collective-permute-start | bytes 196616 | tf_op jit(solution)/shard_map/ppermute | solution.py:32
  3.3 1.8 %copy_bitcast_fusion = (bf16[2,2048,128]{2,1,0:T(8,128)(2,1)S(1)}, bf16[2,2048,128]{2,1,0:T(8,128)(2,1)S(1)}) fusion(bf16[2048,2,128]{2,1,0:T(2,128)(2,1)} %param.8, bf16[2048,2,128]{2,1,0:T(2,128)(2,1)} %param.7), kind=kLoop, calls=%fused_computation | loop fusion | bytes 4194304 | tf_op jit(solution)/shard_map/transpose | solution.py:334
  6.6 4.0 %collective-permute-start.1 = (bf16[2,8,32,128]{3,2,1,0:T(8,128)(2,1)S(1)}, bf16[2,8,32,128]{3,2,1,0:T(8,128)(2,1)S(1)}, u32[]{:S(2)}, u32[]{:S(2)}) collective-permute-start(bf16[2,8,32,128]{3,2,1,0:T(8,128)(2,1)S(1)} %pad_maximum_fusion.refs_0_), channel_id=1, source_target_pairs={{0,64},{1,9},{2,66},{3,11},{4,68},{5,13},{6,70},{7,15},{8,72},{9,1... | collective-permute-start | bytes 393224 | tf_op jit(solution)/shard_map/ppermute | solution.py:32
  11.5 2.2 %collective-permute-start.3 = (bf16[2,8,32,128]{3,2,1,0:T(8,128)(2,1)S(1)}, bf16[2,8,32,128]{3,2,1,0:T(8,128)(2,1)S(1)}, u32[]{:S(2)}, u32[]{:S(2)}) collective-permute-start(bf16[2,8,32,128]{3,2,1,0:T(8,128)(2,1)S(1)} %pad_maximum_fusion.refs_0_), channel_id=1, source_target_pairs={{0,96},{1,13},{2,98},{3,15},{4,100},{5,1},{6,102},{7,3},{8,104},{9... | collective-permute-start | bytes 393224 | tf_op jit(solution)/shard_map/ppermute | solution.py:32
  13.8 2.0 %prepare.1 = (bf16[2,2048,256]{2,1,0:T(8,128)(2,1)S(1)}, bf16[2,2048,256]{2,1,0:T(8,128)(2,1)S(1)}, bf16[2,2048,256]{2,1,0:T(8,128)(2,1)S(1)}, bf16[2,2048,256]{...) custom-call(s32[7]{0:T(128)S(1)} %concatenate.7.info, bf16[2,2048,128]{2,1,0:T(8,128)(2,1)S(1)} %get-tuple-element.29.k_ref, ...), custom_call_target="tpu_custom_call" | custom-call | tf_op jit(solution)/shard_map/prepare/pallas_call | solution.py:97
  17.2 3.1 %collective-permute-start.5 = (bf16[8,8,32,128]{3,2,1,0:T(8,128)(2,1)S(1)}, bf16[8,8,32,128]{3,2,1,0:T(8,128)(2,1)S(1)}, u32[]{:S(2)}, u32[]{:S(2)}) collective-permute-start(bf16[8,8,32,128]{3,2,1,0:T(8,128)(2,1)S(1)} %assemble.3.q_ref), channel_id=1, source_target_pairs={{0,8},{1,65},{2,10},{3,67},{4,12},{5,69},{6,14},{7,71},{8,0},{9,73... | collective-permute-start | bytes 1572872 | tf_op jit(solution)/shard_map/ppermute | solution.py:32
  20.9 2.6 %collective-permute-start.7 = (bf16[8,8,32,128]{3,2,1,0:T(8,128)(2,1)S(1)}, bf16[8,8,32,128]{3,2,1,0:T(8,128)(2,1)S(1)}, u32[]{:S(2)}, u32[]{:S(2)}) collective-permute-start(bf16[8,8,32,128]{3,2,1,0:T(8,128)(2,1)S(1)} %assemble.3.q_ref), channel_id=1, source_target_pairs={{0,12},{1,97},{2,14},{3,99},{4,0},{5,101},{6,2},{7,103},{8,4},{9,1... | collective-permute-start | bytes 1572872 | tf_op jit(solution)/shard_map/ppermute | solution.py:32
  23.6 5.5 %attend_plane.5.refs_0_ = bf16[8,272,128]{2,1,0:T(8,128)(2,1)S(1)} custom-call(bf16[8,8,32,128]{3,2,1,0:T(8,128)(2,1)S(1)} %assemble.3.q_ref, bf16[2,2048,256]{2,1,0:T(8,128)(2,1)S(1)} %get-tuple-element.37.kx, bf16[2,2048,256]{2,1,0:T(8,128)(2,1)S(1)} %get-tuple-element.38.vx), custom_call_target="tpu_custom_call" | custom-call | flops 4294967296 | bytes 4194304 | tf_op jit(solution)/shard_map/attend_plane/pallas_call | solution.py:178
  29.1 4.9 %attend_plane.6 = bf16[8,272,128]{2,1,0:T(8,128)(2,1)S(1)} custom-call(bf16[8,8,32,128]{3,2,1,0:T(8,128)(2,1)S(1)} %collective-permute-done.5.q_ref, bf16[2,2048,256]{2,1,0:T(8,128)(2,1)S(1)} %get-tuple-element.41.kx, bf16[2,2048,256]{2,1,0:T(8,128)(2,1)S(1)} %get-tuple-element.38.vx), custom_call_target="tpu_custom_call" | custom-call | flops 4294967296 | bytes 4194304 | tf_op jit(solution)/shard_map/attend_plane/pallas_call | solution.py:178
  34.1 2.3 %collective-permute-start.9 = (bf16[8,272,128]{2,1,0:T(8,128)(2,1)S(1)}, bf16[8,272,128]{2,1,0:T(8,128)(2,1)S(1)}, u32[]{:S(2)}, u32[]{:S(2)}) collective-permute-start(bf16[8,272,128]{2,1,0:T(8,128)(2,1)S(1)} %attend_plane.6), channel_id=1, source_target_pairs={{0,8},{1,65},{2,10},{3,67},{4,12},{5,69},{6,14},{7,71},{8,0},{9,73... | collective-permute-start | bytes 1671176 | tf_op jit(solution)/shard_map/ppermute | solution.py:32
  36.3 4.9 %attend_plane.7 = bf16[8,272,128]{2,1,0:T(8,128)(2,1)S(1)} custom-call(bf16[8,8,32,128]{3,2,1,0:T(8,128)(2,1)S(1)} %collective-permute-done.6.q_ref, bf16[2,2048,256]{2,1,0:T(8,128)(2,1)S(1)} %get-tuple-element.43.kx, bf16[2,2048,256]{2,1,0:T(8,128)(2,1)S(1)} %get-tuple-element.38.vx), custom_call_target="tpu_custom_call" | custom-call | flops 4294967296 | bytes 4194304 | tf_op jit(solution)/shard_map/attend_plane/pallas_call | solution.py:178
  41.3 1.2 %collective-permute-start.8 = (bf16[8,272,128]{2,1,0:T(8,128)(2,1)S(1)}, bf16[8,272,128]{2,1,0:T(8,128)(2,1)S(1)}, u32[]{:S(2)}, u32[]{:S(2)}) collective-permute-start(bf16[8,272,128]{2,1,0:T(8,128)(2,1)S(1)} %attend_plane.7), channel_id=1, source_target_pairs={{0,12},{1,97},{2,14},{3,99},{4,0},{5,101},{6,2},{7,103},{8,4},{9,1... | collective-permute-start | bytes 1671176 | tf_op jit(solution)/shard_map/ppermute | solution.py:32
  42.5 2.8 %attend_plane.8 = bf16[4,272,128]{2,1,0:T(8,128)(2,1)S(1)} custom-call(bf16[8,8,32,128]{3,2,1,0:T(8,128)(2,1)S(1)} %collective-permute-done.7.q_ref, bf16[2,2048,256]{2,1,0:T(8,128)(2,1)S(1)} %get-tuple-element.46.kx, bf16[2,2048,256]{2,1,0:T(8,128)(2,1)S(1)} %get-tuple-element.38.vx), custom_call_target="tpu_custom_call" | custom-call | flops 2147483648 | bytes 4194304 | tf_op jit(solution)/shard_map/attend_plane/pallas_call | solution.py:178
  46.2 3.0 %attend_plane.9 = bf16[4,272,128]{2,1,0:T(8,128)(2,1)S(1)} custom-call(bf16[8,8,32,128]{3,2,1,0:T(8,128)(2,1)S(1)} %collective-permute-done.7.q_ref, bf16[2,2048,256]{2,1,0:T(8,128)(2,1)S(1)} %get-tuple-element.46.kx, bf16[2,2048,256]{2,1,0:T(8,128)(2,1)S(1)} %get-tuple-element.38.vx), custom_call_target="tpu_custom_call" | custom-call | flops 2147483648 | bytes 4194304 | tf_op jit(solution)/shard_map/attend_plane/pallas_call | solution.py:178
  49.9 3.2 %collective-permute-done.10.refs_3_ = bf16[4,272,128]{2,1,0:T(8,128)(2,1)S(1)} collective-permute-done((bf16[4,272,128]{2,1,0:T(8,128)(2,1)S(1)}, bf16[4,272,128]{2,1,0:T(8,128)(2,1)S(1)}, u32[]{:S(2)}, u32[]{:S(2)}) %collective-permute-start.10) | collective-permute-done | bytes 278560 | tf_op jit(solution)/shard_map/ppermute | solution.py:32
  53.8 1.4 %collective-permute-start.13 = (bf16[2,272,128]{2,1,0:T(8,128)(2,1)S(1)}, bf16[2,272,128]{2,1,0:T(8,128)(2,1)S(1)}, u32[]{:S(2)}, u32[]{:S(2)}) collective-permute-start(bf16[2,272,128]{2,1,0:T(8,128)(2,1)S(1)} %slice.31), channel_id=1, source_target_pairs={{0,64},{1,9},{2,66},{3,11},{4,68},{5,13},{6,70},{7,15},{8,72},{9,1... | collective-permute-start | bytes 417800 | tf_op jit(solution)/shard_map/ppermute | solution.py:32
  55.1 3.1 %collective-permute-done.11.refs_3_ = bf16[4,272,128]{2,1,0:T(8,128)(2,1)S(1)} collective-permute-done((bf16[4,272,128]{2,1,0:T(8,128)(2,1)S(1)}, bf16[4,272,128]{2,1,0:T(8,128)(2,1)S(1)}, u32[]{:S(2)}, u32[]{:S(2)}) %collective-permute-start.11) | collective-permute-done | bytes 278560 | tf_op jit(solution)/shard_map/ppermute | solution.py:32
  59.0 2.1 %collective-permute-start.12 = (bf16[2,272,128]{2,1,0:T(8,128)(2,1)S(1)}, bf16[2,272,128]{2,1,0:T(8,128)(2,1)S(1)}, u32[]{:S(2)}, u32[]{:S(2)}) collective-permute-start(bf16[2,272,128]{2,1,0:T(8,128)(2,1)S(1)} %get-tuple-element.50), channel_id=1, source_target_pairs={{0,96},{1,13},{2,98},{3,15},{4,100},{5,1},{6,102},{7,3},{8,104},{9... | collective-permute-start | bytes 417800 | tf_op jit(solution)/shard_map/ppermute | solution.py:32
  61.1 3.0 %collective-permute-done.12.refs_1_ = bf16[2,272,128]{2,1,0:T(8,128)(2,1)S(1)} collective-permute-done((bf16[2,272,128]{2,1,0:T(8,128)(2,1)S(1)}, bf16[2,272,128]{2,1,0:T(8,128)(2,1)S(1)}, u32[]{:S(2)}, u32[]{:S(2)}) %collective-permute-start.12) | collective-permute-done | bytes 139296 | tf_op jit(solution)/shard_map/ppermute | solution.py:32
  64.1 3.2 %collective-permute-done.14.refs_3_ = bf16[2,272,128]{2,1,0:T(8,128)(2,1)S(1)} collective-permute-done((bf16[2,272,128]{2,1,0:T(8,128)(2,1)S(1)}, bf16[2,272,128]{2,1,0:T(8,128)(2,1)S(1)}, u32[]{:S(2)}, u32[]{:S(2)}) %collective-permute-start.14) | collective-permute-done | bytes 139296 | tf_op jit(solution)/shard_map/ppermute | solution.py:32
  67.7 2.8 %collective-permute-start.15 = (bf16[2,272,128]{2,1,0:T(8,128)(2,1)S(1)}, bf16[2,272,128]{2,1,0:T(8,128)(2,1)S(1)}, u32[]{:S(2)}, u32[]{:S(2)}) collective-permute-start(bf16[2,272,128]{2,1,0:T(8,128)(2,1)S(1)} %combine.5.mine), channel_id=1, source_target_pairs={{0,16},{1,17},{2,18},{3,19},{4,20},{5,21},{6,22},{7,23},{8,24},{9,... | collective-permute-start | bytes 417800 | tf_op jit(solution)/shard_map/ppermute | solution.py:32
  70.5 3.8 %collective-permute-done.15.theirs = bf16[2,272,128]{2,1,0:T(8,128)(2,1)S(1)} collective-permute-done((bf16[2,272,128]{2,1,0:T(8,128)(2,1)S(1)}, bf16[2,272,128]{2,1,0:T(8,128)(2,1)S(1)}, u32[]{:S(2)}, u32[]{:S(2)}) %collective-permute-start.15) | collective-permute-done | bytes 139296 | tf_op jit(solution)/shard_map/ppermute | solution.py:32
  74.8 1.5 %collective-permute-start.19 = (bf16[16,4096]{1,0:T(8,128)(2,1)S(1)}, bf16[16,4096]{1,0:T(8,128)(2,1)S(1)}, u32[]{:S(2)}, u32[]{:S(2)}) collective-permute-start(bf16[16,4096]{1,0:T(8,128)(2,1)S(1)} %finish.1.refs_0_), channel_id=1, source_target_pairs={{0,96},{1,13},{2,98},{3,15},{4,100},{5,1},{6,102},{7,3},{8,104},{9... | collective-permute-start | bytes 393224 | tf_op jit(solution)/shard_map/ppermute | solution.py:32
  76.9 4.4 %collective-permute-done.17.refs_0_ = bf16[16,4096]{1,0:T(8,128)(2,1)S(1)} collective-permute-done((bf16[16,4096]{1,0:T(8,128)(2,1)S(1)}, bf16[16,4096]{1,0:T(8,128)(2,1)S(1)}, u32[]{:S(2)}, u32[]{:S(2)}) %collective-permute-start.17) | collective-permute-done | bytes 131104 | tf_op jit(solution)/shard_map/ppermute | solution.py:32
  83.5 2.5 %collective-permute-start.22 = (bf16[32,4096]{1,0:T(8,128)(2,1)S(1)}, bf16[32,4096]{1,0:T(8,128)(2,1)S(1)}, u32[]{:S(2)}, u32[]{:S(2)}) collective-permute-start(bf16[32,4096]{1,0:T(8,128)(2,1)S(1)} %assemble.4.xa), channel_id=1, source_target_pairs={{0,12},{1,97},{2,14},{3,99},{4,0},{5,101},{6,2},{7,103},{8,4},{9,1... | collective-permute-start | bytes 786440 | tf_op jit(solution)/shard_map/ppermute | solution.py:32
  86.0 1.8 %collective-permute-done.23.xb = bf16[32,4096]{1,0:T(8,128)(2,1)S(1)} collective-permute-done((bf16[32,4096]{1,0:T(8,128)(2,1)S(1)}, bf16[32,4096]{1,0:T(8,128)(2,1)S(1)}, u32[]{:S(2)}, u32[]{:S(2)}) %collective-permute-start.23) | collective-permute-done | bytes 262176 | tf_op jit(solution)/shard_map/ppermute | solution.py:32
  87.7 2.3 %collective-permute-start.25 = (bf16[32,4096]{1,0:T(8,128)(2,1)S(1)}, bf16[32,4096]{1,0:T(8,128)(2,1)S(1)}, u32[]{:S(2)}, u32[]{:S(2)}) collective-permute-start(bf16[32,4096]{1,0:T(8,128)(2,1)S(1)} %collective-permute-done.23.xb), channel_id=1, source_target_pairs={{0,12},{1,97},{2,14},{3,99},{4,0},{5,101},{6,2},{7,103},{8,4},{9,1... | collective-permute-start | bytes 786440 | tf_op jit(solution)/shard_map/ppermute | solution.py:32
  92.1 1.5 %collective-permute-done.21.xb = bf16[32,4096]{1,0:T(8,128)(2,1)S(1)} collective-permute-done((bf16[32,4096]{1,0:T(8,128)(2,1)S(1)}, bf16[32,4096]{1,0:T(8,128)(2,1)S(1)}, u32[]{:S(2)}, u32[]{:S(2)}) %collective-permute-start.21) | collective-permute-done | bytes 262176 | tf_op jit(solution)/shard_map/ppermute | solution.py:32
  94.4 3.5 %collective-permute-done.24.xa = bf16[32,4096]{1,0:T(8,128)(2,1)S(1)} collective-permute-done((bf16[32,4096]{1,0:T(8,128)(2,1)S(1)}, bf16[32,4096]{1,0:T(8,128)(2,1)S(1)}, u32[]{:S(2)}, u32[]{:S(2)}) %collective-permute-start.24) | collective-permute-done | bytes 262176 | tf_op jit(solution)/shard_map/ppermute | solution.py:32
  97.9 1.4 %place.1 = f32[256,512]{1,0:T(8,128)S(1)} custom-call(s32[7]{0:T(128)S(1)} %concatenate.7.info, f32[64,512]{1,0:T(8,128)S(1)} %project.3.y0, f32[64,512]{1,0:T(8,128)S(1)} %project.4.y1, f32[64,512]{1,0:T(8,128)S(1)} %project.5.y3, bf16[32,4096]{1,0:T(8,128)(2,1)S(1)} %collective-permute-done.24.xa, bf16[32,4096]{1,0:T(8,128)(2,1)S(1)} %collective-permute-done.25.xb, ...), custom_call_target="tpu_custom_call" | custom-call | tf_op jit(solution)/shard_map/place/pallas_call | solution.py:319
  99.4 1.3 %collective-permute-done.26 = bf16[128,512]{1,0:T(8,128)(2,1)S(1)} collective-permute-done((bf16[128,512]{1,0:T(8,128)(2,1)S(1)}, bf16[128,512]{1,0:T(8,128)(2,1)S(1)}, u32[]{:S(2)}, u32[]{:S(2)}) %collective-permute-start.26) | collective-permute-done | bytes 131104 | tf_op jit(solution)/shard_map/ppermute | solution.py:32
  102.0 3.2 %collective-permute-done.27 = bf16[64,512]{1,0:T(8,128)(2,1)S(1)} collective-permute-done((bf16[64,512]{1,0:T(8,128)(2,1)S(1)}, bf16[64,512]{1,0:T(8,128)(2,1)S(1)}, u32[]{:S(2)}, u32[]{:S(2)}) %collective-permute-start.27) | collective-permute-done | bytes 65568 | tf_op jit(solution)/shard_map/ppermute | solution.py:32
  (54 shorter events, 14.6 us)
Async XLA Ops:
  0.0 6.5 %copy-start.1 = (bf16[8,32,128]{2,1,0:T(8,128)(2,1)S(1)}, bf16[8,32,128]{2,1,0:T(8,128)(2,1)}, u32[]{:S(2)}) copy-start(bf16[8,32,128]{2,1,0:T(8,128)(2,1)} %param.6) | copy-start | bytes 196612
  0.0 6.5 %collective-permute-start = (bf16[1,8,32,128]{3,2,1,0:T(8,128)(2,1)}, bf16[1,8,32,128]{3,2,1,0:T(8,128)(2,1)S(1)}, u32[]{:S(2)}, u32[]{:S(2)}) collective-permute-start(bf16[1,8,32,128]{3,2,1,0:T(8,128)(2,1)} %bitcast.10), channel_id=1, source_target_pairs={{0,16},{1,17},{2,18},{3,19},{4,20},{5,21},{6,22},{7,23},{8,24},{9,... | collective-permute-start | bytes 196616 | tf_op jit(solution)/shard_map/ppermute | solution.py:32
  6.6 9.2 %collective-permute-start.1 = (bf16[2,8,32,128]{3,2,1,0:T(8,128)(2,1)S(1)}, bf16[2,8,32,128]{3,2,1,0:T(8,128)(2,1)S(1)}, u32[]{:S(2)}, u32[]{:S(2)}) collective-permute-start(bf16[2,8,32,128]{3,2,1,0:T(8,128)(2,1)S(1)} %pad_maximum_fusion.refs_0_), channel_id=1, source_target_pairs={{0,64},{1,9},{2,66},{3,11},{4,68},{5,13},{6,70},{7,15},{8,72},{9,1... | collective-permute-start | bytes 393224 | tf_op jit(solution)/shard_map/ppermute | solution.py:32
  10.5 6.2 %collective-permute-start.2 = (bf16[2,8,32,128]{3,2,1,0:T(8,128)(2,1)S(1)}, bf16[2,8,32,128]{3,2,1,0:T(8,128)(2,1)S(1)}, u32[]{:S(2)}, u32[]{:S(2)}) collective-permute-start(bf16[2,8,32,128]{3,2,1,0:T(8,128)(2,1)S(1)} %pad_maximum_fusion.refs_0_), channel_id=1, source_target_pairs={{0,32},{1,5},{2,34},{3,7},{4,36},{5,9},{6,38},{7,11},{8,40},{9,13}... | collective-permute-start | bytes 393224 | tf_op jit(solution)/shard_map/ppermute | solution.py:32
  11.5 5.2 %collective-permute-start.3 = (bf16[2,8,32,128]{3,2,1,0:T(8,128)(2,1)S(1)}, bf16[2,8,32,128]{3,2,1,0:T(8,128)(2,1)S(1)}, u32[]{:S(2)}, u32[]{:S(2)}) collective-permute-start(bf16[2,8,32,128]{3,2,1,0:T(8,128)(2,1)S(1)} %pad_maximum_fusion.refs_0_), channel_id=1, source_target_pairs={{0,96},{1,13},{2,98},{3,15},{4,100},{5,1},{6,102},{7,3},{8,104},{9... | collective-permute-start | bytes 393224 | tf_op jit(solution)/shard_map/ppermute | solution.py:32
  15.7 1.4 %collective-permute-start.4 = (bf16[2,8,32,128]{3,2,1,0:T(8,128)(2,1)S(1)}, bf16[2,8,32,128]{3,2,1,0:T(8,128)(2,1)S(1)}, u32[]{:S(2)}, u32[]{:S(2)}) collective-permute-start(bf16[2,8,32,128]{3,2,1,0:T(8,128)(2,1)S(1)} %collective-permute-done.1.refs_1_), channel_id=1, source_target_pairs={{0,1},{1,0},{2,3},{3,2},{4,5},{5,4},{6,7},{7,6},{8,9},{9,8},{10,11... | collective-permute-start | bytes 393224 | tf_op jit(solution)/shard_map/ppermute | solution.py:32
  17.2 11.9 %collective-permute-start.5 = (bf16[8,8,32,128]{3,2,1,0:T(8,128)(2,1)S(1)}, bf16[8,8,32,128]{3,2,1,0:T(8,128)(2,1)S(1)}, u32[]{:S(2)}, u32[]{:S(2)}) collective-permute-start(bf16[8,8,32,128]{3,2,1,0:T(8,128)(2,1)S(1)} %assemble.3.q_ref), channel_id=1, source_target_pairs={{0,8},{1,65},{2,10},{3,67},{4,12},{5,69},{6,14},{7,71},{8,0},{9,73... | collective-permute-start | bytes 1572872 | tf_op jit(solution)/shard_map/ppermute | solution.py:32
  20.3 16.0 %collective-permute-start.6 = (bf16[8,8,32,128]{3,2,1,0:T(8,128)(2,1)S(1)}, bf16[8,8,32,128]{3,2,1,0:T(8,128)(2,1)S(1)}, u32[]{:S(2)}, u32[]{:S(2)}) collective-permute-start(bf16[8,8,32,128]{3,2,1,0:T(8,128)(2,1)S(1)} %assemble.3.q_ref), channel_id=1, source_target_pairs={{0,4},{1,33},{2,6},{3,35},{4,8},{5,37},{6,10},{7,39},{8,12},{9,41}... | collective-permute-start | bytes 1572872 | tf_op jit(solution)/shard_map/ppermute | solution.py:32
  20.9 15.4 %collective-permute-start.7 = (bf16[8,8,32,128]{3,2,1,0:T(8,128)(2,1)S(1)}, bf16[8,8,32,128]{3,2,1,0:T(8,128)(2,1)S(1)}, u32[]{:S(2)}, u32[]{:S(2)}) collective-permute-start(bf16[8,8,32,128]{3,2,1,0:T(8,128)(2,1)S(1)} %assemble.3.q_ref), channel_id=1, source_target_pairs={{0,12},{1,97},{2,14},{3,99},{4,0},{5,101},{6,2},{7,103},{8,4},{9,1... | collective-permute-start | bytes 1572872 | tf_op jit(solution)/shard_map/ppermute | solution.py:32
  34.1 12.1 %collective-permute-start.9 = (bf16[8,272,128]{2,1,0:T(8,128)(2,1)S(1)}, bf16[8,272,128]{2,1,0:T(8,128)(2,1)S(1)}, u32[]{:S(2)}, u32[]{:S(2)}) collective-permute-start(bf16[8,272,128]{2,1,0:T(8,128)(2,1)S(1)} %attend_plane.6), channel_id=1, source_target_pairs={{0,8},{1,65},{2,10},{3,67},{4,12},{5,69},{6,14},{7,71},{8,0},{9,73... | collective-permute-start | bytes 1671176 | tf_op jit(solution)/shard_map/ppermute | solution.py:32
  41.3 11.8 %collective-permute-start.8 = (bf16[8,272,128]{2,1,0:T(8,128)(2,1)S(1)}, bf16[8,272,128]{2,1,0:T(8,128)(2,1)S(1)}, u32[]{:S(2)}, u32[]{:S(2)}) collective-permute-start(bf16[8,272,128]{2,1,0:T(8,128)(2,1)S(1)} %attend_plane.7), channel_id=1, source_target_pairs={{0,12},{1,97},{2,14},{3,99},{4,0},{5,101},{6,2},{7,103},{8,4},{9,1... | collective-permute-start | bytes 1671176 | tf_op jit(solution)/shard_map/ppermute | solution.py:32
  45.2 7.8 %collective-permute-start.10 = (bf16[4,272,128]{2,1,0:T(8,128)(2,1)S(1)}, bf16[4,272,128]{2,1,0:T(8,128)(2,1)S(1)}, u32[]{:S(2)}, u32[]{:S(2)}) collective-permute-start(bf16[4,272,128]{2,1,0:T(8,128)(2,1)S(1)} %attend_plane.8), channel_id=1, source_target_pairs={{0,4},{1,33},{2,6},{3,35},{4,8},{5,37},{6,10},{7,39},{8,12},{9,41}... | collective-permute-start | bytes 835592 | tf_op jit(solution)/shard_map/ppermute | solution.py:32
  49.2 9.1 %collective-permute-start.11 = (bf16[4,272,128]{2,1,0:T(8,128)(2,1)S(1)}, bf16[4,272,128]{2,1,0:T(8,128)(2,1)S(1)}, u32[]{:S(2)}, u32[]{:S(2)}) collective-permute-start(bf16[4,272,128]{2,1,0:T(8,128)(2,1)S(1)} %attend_plane.9), channel_id=1, source_target_pairs={{0,4},{1,33},{2,6},{3,35},{4,8},{5,37},{6,10},{7,39},{8,12},{9,41}... | collective-permute-start | bytes 835592 | tf_op jit(solution)/shard_map/ppermute | solution.py:32
  53.8 36.6 %copy-start = (bf16[4096,512]{1,0:T(8,128)(2,1)S(1)}, bf16[4096,512]{1,0:T(8,128)(2,1)}, u32[]{:S(2)}) copy-start(bf16[4096,512]{1,0:T(8,128)(2,1)} %w_ref.7) | copy-start | bytes 12582916
  53.8 7.3 %collective-permute-start.13 = (bf16[2,272,128]{2,1,0:T(8,128)(2,1)S(1)}, bf16[2,272,128]{2,1,0:T(8,128)(2,1)S(1)}, u32[]{:S(2)}, u32[]{:S(2)}) collective-permute-start(bf16[2,272,128]{2,1,0:T(8,128)(2,1)S(1)} %slice.31), channel_id=1, source_target_pairs={{0,64},{1,9},{2,66},{3,11},{4,68},{5,13},{6,70},{7,15},{8,72},{9,1... | collective-permute-start | bytes 417800 | tf_op jit(solution)/shard_map/ppermute | solution.py:32
  59.0 5.1 %collective-permute-start.12 = (bf16[2,272,128]{2,1,0:T(8,128)(2,1)S(1)}, bf16[2,272,128]{2,1,0:T(8,128)(2,1)S(1)}, u32[]{:S(2)}, u32[]{:S(2)}) collective-permute-start(bf16[2,272,128]{2,1,0:T(8,128)(2,1)S(1)} %get-tuple-element.50), channel_id=1, source_target_pairs={{0,96},{1,13},{2,98},{3,15},{4,100},{5,1},{6,102},{7,3},{8,104},{9... | collective-permute-start | bytes 417800 | tf_op jit(solution)/shard_map/ppermute | solution.py:32
  61.1 6.3 %collective-permute-start.14 = (bf16[2,272,128]{2,1,0:T(8,128)(2,1)S(1)}, bf16[2,272,128]{2,1,0:T(8,128)(2,1)S(1)}, u32[]{:S(2)}, u32[]{:S(2)}) collective-permute-start(bf16[2,272,128]{2,1,0:T(8,128)(2,1)S(1)} %get-tuple-element.49), channel_id=1, source_target_pairs={{0,32},{1,5},{2,34},{3,7},{4,36},{5,9},{6,38},{7,11},{8,40},{9,13}... | collective-permute-start | bytes 417800 | tf_op jit(solution)/shard_map/ppermute | solution.py:32
  67.7 6.6 %collective-permute-start.15 = (bf16[2,272,128]{2,1,0:T(8,128)(2,1)S(1)}, bf16[2,272,128]{2,1,0:T(8,128)(2,1)S(1)}, u32[]{:S(2)}, u32[]{:S(2)}) collective-permute-start(bf16[2,272,128]{2,1,0:T(8,128)(2,1)S(1)} %combine.5.mine), channel_id=1, source_target_pairs={{0,16},{1,17},{2,18},{3,19},{4,20},{5,21},{6,22},{7,23},{8,24},{9,... | collective-permute-start | bytes 417800 | tf_op jit(solution)/shard_map/ppermute | solution.py:32
  74.7 6.6 %collective-permute-start.17 = (bf16[16,4096]{1,0:T(8,128)(2,1)S(1)}, bf16[16,4096]{1,0:T(8,128)(2,1)S(1)}, u32[]{:S(2)}, u32[]{:S(2)}) collective-permute-start(bf16[16,4096]{1,0:T(8,128)(2,1)S(1)} %finish.1.refs_0_), channel_id=1, source_target_pairs={{0,64},{1,9},{2,66},{3,11},{4,68},{5,13},{6,70},{7,15},{8,72},{9,1... | collective-permute-start | bytes 393224 | tf_op jit(solution)/shard_map/ppermute | solution.py:32
  74.8 6.5 %collective-permute-start.19 = (bf16[16,4096]{1,0:T(8,128)(2,1)S(1)}, bf16[16,4096]{1,0:T(8,128)(2,1)S(1)}, u32[]{:S(2)}, u32[]{:S(2)}) collective-permute-start(bf16[16,4096]{1,0:T(8,128)(2,1)S(1)} %finish.1.refs_0_), channel_id=1, source_target_pairs={{0,96},{1,13},{2,98},{3,15},{4,100},{5,1},{6,102},{7,3},{8,104},{9... | collective-permute-start | bytes 393224 | tf_op jit(solution)/shard_map/ppermute | solution.py:32
  76.2 6.4 %collective-permute-start.16 = (bf16[16,4096]{1,0:T(8,128)(2,1)S(1)}, bf16[16,4096]{1,0:T(8,128)(2,1)S(1)}, u32[]{:S(2)}, u32[]{:S(2)}) collective-permute-start(bf16[16,4096]{1,0:T(8,128)(2,1)S(1)} %finish.1.refs_0_), channel_id=1, source_target_pairs={{0,32},{1,5},{2,34},{3,7},{4,36},{5,9},{6,38},{7,11},{8,40},{9,13}... | collective-permute-start | bytes 393224 | tf_op jit(solution)/shard_map/ppermute | solution.py:32
  81.3 1.4 %collective-permute-start.18 = (bf16[16,4096]{1,0:T(8,128)(2,1)S(1)}, bf16[16,4096]{1,0:T(8,128)(2,1)S(1)}, u32[]{:S(2)}, u32[]{:S(2)}) collective-permute-start(bf16[16,4096]{1,0:T(8,128)(2,1)S(1)} %collective-permute-done.17.refs_0_), channel_id=1, source_target_pairs={{0,1},{1,0},{2,3},{3,2},{4,5},{5,4},{6,7},{7,6},{8,9},{9,8},{10,11... | collective-permute-start | bytes 393224 | tf_op jit(solution)/shard_map/ppermute | solution.py:32
  81.3 6.4 %collective-permute-start.23 = (bf16[32,4096]{1,0:T(8,128)(2,1)S(1)}, bf16[32,4096]{1,0:T(8,128)(2,1)S(1)}, u32[]{:S(2)}, u32[]{:S(2)}) collective-permute-start(bf16[32,4096]{1,0:T(8,128)(2,1)S(1)} %assemble.5.xb), channel_id=1, source_target_pairs={{0,12},{1,97},{2,14},{3,99},{4,0},{5,101},{6,2},{7,103},{8,4},{9,1... | collective-permute-start | bytes 786440 | tf_op jit(solution)/shard_map/ppermute | solution.py:32
  82.7 7.7 %collective-permute-start.20 = (bf16[32,4096]{1,0:T(8,128)(2,1)S(1)}, bf16[32,4096]{1,0:T(8,128)(2,1)S(1)}, u32[]{:S(2)}, u32[]{:S(2)}) collective-permute-start(bf16[32,4096]{1,0:T(8,128)(2,1)S(1)} %assemble.4.xa), channel_id=1, source_target_pairs={{0,4},{1,33},{2,6},{3,35},{4,8},{5,37},{6,10},{7,39},{8,12},{9,41}... | collective-permute-start | bytes 786440 | tf_op jit(solution)/shard_map/ppermute | solution.py:32
  83.5 7.7 %collective-permute-start.22 = (bf16[32,4096]{1,0:T(8,128)(2,1)S(1)}, bf16[32,4096]{1,0:T(8,128)(2,1)S(1)}, u32[]{:S(2)}, u32[]{:S(2)}) collective-permute-start(bf16[32,4096]{1,0:T(8,128)(2,1)S(1)} %assemble.4.xa), channel_id=1, source_target_pairs={{0,12},{1,97},{2,14},{3,99},{4,0},{5,101},{6,2},{7,103},{8,4},{9,1... | collective-permute-start | bytes 786440 | tf_op jit(solution)/shard_map/ppermute | solution.py:32
  86.0 7.6 %collective-permute-start.21 = (bf16[32,4096]{1,0:T(8,128)(2,1)S(1)}, bf16[32,4096]{1,0:T(8,128)(2,1)S(1)}, u32[]{:S(2)}, u32[]{:S(2)}) collective-permute-start(bf16[32,4096]{1,0:T(8,128)(2,1)S(1)} %assemble.5.xb), channel_id=1, source_target_pairs={{0,4},{1,33},{2,6},{3,35},{4,8},{5,37},{6,10},{7,39},{8,12},{9,41}... | collective-permute-start | bytes 786440 | tf_op jit(solution)/shard_map/ppermute | solution.py:32
  87.7 6.7 %collective-permute-start.25 = (bf16[32,4096]{1,0:T(8,128)(2,1)S(1)}, bf16[32,4096]{1,0:T(8,128)(2,1)S(1)}, u32[]{:S(2)}, u32[]{:S(2)}) collective-permute-start(bf16[32,4096]{1,0:T(8,128)(2,1)S(1)} %collective-permute-done.23.xb), channel_id=1, source_target_pairs={{0,12},{1,97},{2,14},{3,99},{4,0},{5,101},{6,2},{7,103},{8,4},{9,1... | collective-permute-start | bytes 786440 | tf_op jit(solution)/shard_map/ppermute | solution.py:32
  90.3 7.6 %collective-permute-start.24 = (bf16[32,4096]{1,0:T(8,128)(2,1)S(1)}, bf16[32,4096]{1,0:T(8,128)(2,1)S(1)}, u32[]{:S(2)}, u32[]{:S(2)}) collective-permute-start(bf16[32,4096]{1,0:T(8,128)(2,1)S(1)} %collective-permute-done.20.xa), channel_id=1, source_target_pairs={{0,4},{1,33},{2,6},{3,35},{4,8},{5,37},{6,10},{7,39},{8,12},{9,41}... | collective-permute-start | bytes 786440 | tf_op jit(solution)/shard_map/ppermute | solution.py:32
  99.3 1.4 %collective-permute-start.26 = (bf16[128,512]{1,0:T(8,128)(2,1)S(1)}, bf16[128,512]{1,0:T(8,128)(2,1)S(1)}, u32[]{:S(2)}, u32[]{:S(2)}) collective-permute-start(bf16[128,512]{1,0:T(8,128)(2,1)S(1)} %slice.43), channel_id=1, source_target_pairs={{0,1},{1,0},{2,3},{3,2},{4,5},{5,4},{6,7},{7,6},{8,9},{9,8},{10,11... | collective-permute-start | bytes 393224 | tf_op jit(solution)/shard_map/ppermute | solution.py:32
  100.8 4.3 %collective-permute-start.27 = (bf16[64,512]{1,0:T(8,128)(2,1)S(1)}, bf16[64,512]{1,0:T(8,128)(2,1)S(1)}, u32[]{:S(2)}, u32[]{:S(2)}) collective-permute-start(bf16[64,512]{1,0:T(8,128)(2,1)S(1)} %slice.44), channel_id=1, source_target_pairs={{0,2},{1,3},{2,0},{3,1},{4,6},{5,7},{6,4},{7,5},{8,10},{9,11},{10,... | collective-permute-start | bytes 196616 | tf_op jit(solution)/shard_map/ppermute | solution.py:32
